TPU v7x, 32 devices: a whole 2x2x4 slice. The times are simulated.
32 devices in a mesh: col: 16 (over z, y, x), row: 2 (over core).
Axes of the slice: x: 2, y: 2, z: 4, core: 2. Of those that a mesh axis runs over, the one named last changes fastest.
Arguments:
- slab_embed: float32 [64, 1024], P(None, 'row'), may hold values from -6 to 6
- slab_probe: float32 [32, 1024], P(None, 'row'), may hold values from -6 to 6
- point_embed: float32 [64, 32768], P(None, 'col'), may hold values from -6 to 6
- point_probe: float32 [32, 32768], P(None, 'col'), may hold values from -1.2 to 1.2
- inv_scale: float32 [64], replicated, may hold values from 0.08 to 0.3
Outputs:
- slab_grad: float32 [64, 1024], P(None, 'row')
- point_grad: float32 [64, 32768], P(None, 'col')
All inputs are finite; a program needn't handle non-finite values.
Results may differ from a plain program's by a relative error of at most 0.0001.
Values sent between devices are 32-bit elements; how exact they have to be, the bound alone decides.
No kernel may reach another device: no remote copies, remote signals or barrier semaphores. Data moves between devices by JAX's collectives and lax.ppermute only.
A program may use at most 64 MiB of HBM per device.

v0:
```python
import jax
import jax.numpy as jnp
from jax import lax
from jax.sharding import PartitionSpec as P


def local(slab_embed, slab_probe, point_embed, point_probe, inv_scale):
    hp = lax.Precision.HIGHEST
    weight_sq = inv_scale * inv_scale
    scaled = slab_embed * weight_sq[:, None]
    self_term = jnp.sum(scaled * slab_embed, axis=0)
    points_here = point_embed.shape[1]
    width = min(1024, points_here)
    row_total = jnp.zeros((slab_embed.shape[1],), jnp.float32)
    mixed = jnp.zeros(slab_embed.shape, jnp.float32)
    pieces = []
    for block in range(points_here // width):
        points = point_embed[:, block * width : (block + 1) * width]
        probes = point_probe[:, block * width : (block + 1) * width]
        other_term = jnp.sum(weight_sq[:, None] * points * points, axis=0)
        cross = jnp.dot(scaled.T, points, precision=hp)
        kernel = jnp.exp(-0.5 * (self_term[:, None] + other_term[None, :] - 2.0 * cross))
        weights = kernel * jnp.dot(slab_probe.T, probes, precision=hp)
        row_total = row_total + jnp.sum(weights, axis=1)
        mixed = mixed + jnp.dot(points, weights.T, precision=hp)
        pieces.append(
            weight_sq[:, None]
            * (
                jnp.dot(slab_embed, weights, precision=hp)
                - points * jnp.sum(weights, axis=0)[None, :]
            )
        )
    slab_terms = -weight_sq[:, None] * (slab_embed * row_total[None, :] - mixed)
    point_terms = jnp.concatenate(pieces, axis=1)
    slab_grad = lax.psum(slab_terms, "col")
    point_grad = lax.psum(point_terms, "row")
    return (slab_grad, point_grad)


def solution(mesh):
    placed = (P(None, "row"), P(None, "row"), P(None, "col"), P(None, "col"), P())
    return jax.shard_map(
        local,
        mesh=mesh,
        in_specs=placed,
        out_specs=(P(None, "row"), P(None, "col")),
        check_vma=False,
    )
```

profile of v0, /device:TPU:0, one launch (start us, length us, event | category | flops | bytes accessed | tf_op | source)
XLA Modules:
  0.0 164.3 jit_solution(8622586809294703536)
XLA Ops:
  7.2 0.0 copy-start
  7.2 0.0 copy-start.4
  7.2 0.0 copy-start.3
  7.2 0.0 all-reduce.3.cloned.1.call-start
  7.2 0.7 multiply_negate_fusion
  8.0 1.0 fusion.18
  9.0 1.2 fusion.8
  10.2 0.0 copy-start.5
  10.2 3.0 %fusion.14 = f32[512,1024]{1,0:T(8,128)S(1)} fusion(f32[64,2048]{1,0:T(8,128)} %param.7, f32[64,512]{1,0:T(8,128)} %param.5, f32[64]{0:T(128)S(1)} %get-tuple-element.9), kind=kOutput, calls=%fused_computation.22 | convolution fusion | flops 402685952 | bytes 2490624 | tf_op jit(solution)/shard_map/dot_general | solution.py:21
  13.2 0.0 copy-done.4
  13.2 0.0 copy-done.3
  13.2 1.9 %fusion.10 = f32[512,1024]{1,0:T(8,128)S(1)} fusion(f32[64,2048]{1,0:T(8,128)S(1)} %copy-done.3, f32[64,512]{1,0:T(8,128)S(1)} %copy-done.4, f32[64]{0:T(128)S(1)} %get-tuple-element.9), kind=kOutput, calls=%fused_computation.18 | convolution fusion | flops 402685952 | bytes 2490880 | tf_op jit(solution)/shard_map/dot_general | solution.py:21
  15.1 0.0 copy-done
  15.1 0.0 copy-done.5
  15.1 2.4 %fusion.23 = (f32[1024]{0:T(1024)S(1)}, f32[512]{0:T(512)S(1)}, f32[512,1024]{1,0:T(8,128)S(1)}) fusion(f32[32,512]{1,0:T(8,128)S(1)} %copy-done, f32[32,2048]{1,0:T(8,128)S(1)} %copy-done.5, f32[512,1024]{1,0:T(8,128)S(1)} %fusion.14, f32[1024]{0:T(1024)S(1)} %get-tuple-element.7, f32[512]{0:T(512)S(1)} %fusion.18), kind=kOutput, calls=%fused_computation.33 | convolution fusion | flops 204995072 | bytes 4403200 | tf_op jit(solution)/shard_map/dot_general | solution.py:23
  17.5 2.2 %fusion.12 = f32[512,64]{0,1:T(8,128)S(1)} fusion(f32[512,1024]{1,0:T(8,128)S(1)} %get-tuple-element.10, f32[64,2048]{1,0:T(8,128)S(1)} %copy-done.3), kind=kOutput, calls=%fused_computation.20 | convolution fusion | flops 402653184 | bytes 2490368 | tf_op jit(solution)/shard_map/dot_general | solution.py:25
  19.7 2.4 %fusion.24 = (f32[1024]{0:T(1024)S(1)}, f32[512]{0:T(512)S(1)}, f32[512,1024]{1,0:T(8,128)S(1)}) fusion(f32[32,512]{1,0:T(8,128)S(1)} %copy-done, f32[32,2048]{1,0:T(8,128)S(1)} %copy-done.5, f32[512,1024]{1,0:T(8,128)S(1)} %fusion.10, f32[1024]{0:T(1024)S(1)} %get-tuple-element.6, f32[512]{0:T(512)S(1)} %fusion.18), kind=kOutput, calls=%fused_computation.34 | convolution fusion | flops 204995072 | bytes 4403200 | tf_op jit(solution)/shard_map/dot_general | solution.py:23
  22.0 0.0 copy-start.1
  22.1 1.3 copy-done.1
  23.4 2.8 %fusion.6 = f32[64,512]{1,0:T(8,128)} fusion(f32[512,64]{0,1:T(8,128)S(1)} %fusion.12, f32[512,1024]{1,0:T(8,128)S(1)} %get-tuple-element.11, f32[64,2048]{1,0:T(8,128)S(1)} %copy-done.3, f32[64,512]{1,0:T(8,128)S(1)} %copy-done.4, f32[512]{0:T(512)S(1)} %add.46, f32[64]{0:T(128)S(1)} %get-tuple-element.8), kind=kOutput, calls=%fused_computation.11 | convolution fusion | flops 402784256 | bytes 2755072 | tf_op jit(solution)/shard_map/dot_general | solution.py:25
  26.2 0.0 all-reduce.3.cloned.1.call-update
  26.2 0.2 all-reduce.5.cloned.1.call-start
  26.5 0.0 copy-start.2
  26.5 1.5 fusion.3
  27.9 0.1 copy-done.2
  28.1 1.5 fusion.1
  29.5 0.8 pad_maximum_fusion
  30.4 0.0 all-reduce.5.cloned.1.call-update
  30.4 102.9 %all-reduce.3.cloned.1.call-done = f32[64,512]{1,0:T(8,128)} async-done(((f32[64,512]{1,0:T(8,128)}), f32[64,512]{1,0:T(8,128)}) %all-reduce.3.cloned.1.call-update) | async-done | bytes 131088 | tf_op jit(solution)/shard_map/psum | solution.py:35
  133.3 20.7 %all-reduce.5.cloned.1.call-done = f32[64,2048]{1,0:T(8,128)} async-done(((f32[64,2048]{1,0:T(8,128)}), f32[64,2048]{1,0:T(8,128)}) %all-reduce.5.cloned.1.call-update) | async-done | bytes 524304 | tf_op jit(solution)/shard_map/psum | solution.py:36
  154.0 1.6 copy.9
  155.5 1.9 %copy.10 = f32[64,2048]{1,0:T(8,128)} copy(f32[64,2048]{1,0:T(8,128)} %all-reduce.5.cloned.1.call-done) | data formatting | bytes 1048576
  (1 shorter events, 0.0 us)
Async XLA Ops:
  7.2 7.9 %copy-start = (f32[32,512]{1,0:T(8,128)S(1)}, f32[32,512]{1,0:T(8,128)}, u32[]{:S(2)}) copy-start(f32[32,512]{1,0:T(8,128)} %param.6) | copy-start | bytes 196612
  7.2 6.0 %copy-start.4 = (f32[64,512]{1,0:T(8,128)S(1)}, f32[64,512]{1,0:T(8,128)}, u32[]{:S(2)}) copy-start(f32[64,512]{1,0:T(8,128)} %param.5) | copy-start | bytes 393220
  7.2 6.0 %copy-start.3 = (f32[64,2048]{1,0:T(8,128)S(1)}, f32[64,2048]{1,0:T(8,128)}, u32[]{:S(2)}) copy-start(f32[64,2048]{1,0:T(8,128)} %param.7) | copy-start | bytes 1572868
  7.2 126.1 %all-reduce.3.cloned.1.call-start = ((), (), s32[]{:S(2)}) async-start(), calls=%async_computation | async-start | bytes 262144 | tf_op jit(solution)/shard_map/psum | solution.py:35
  10.2 4.9 %copy-start.5 = (f32[32,2048]{1,0:T(8,128)S(1)}, f32[32,2048]{1,0:T(8,128)}, u32[]{:S(2)}) copy-start(f32[32,2048]{1,0:T(8,128)} %param.8) | copy-start | bytes 786436
  22.0 1.4 copy-start.1
  26.2 127.7 %all-reduce.5.cloned.1.call-start = ((), (), s32[]{:S(2)}) async-start(), calls=%async_computation.1 | async-start | bytes 1048576 | tf_op jit(solution)/shard_map/psum | solution.py:36
  26.5 1.6 copy-start.2
Sparse Core Ops, SparseCore 0:
  26.4 106.8 all-reduce.2
  136.2 17.7 all-reduce.4
where the time goes:
time: 165 us; the launch traced here: 164 us
  waiting for transfers between devices  124 us (75%)
  matrix products  17.5 us (11%)
  between operations  14.1 us (9%)
  local copies, waits for them, and re-layouts  4.94 us (3%)
  other arithmetic  3.75 us (2%)
    psum x1, waiting for transfers between devices, local(): slab_grad = lax.psum(slab_terms, 'col')  103 us
    psum x1, waiting for transfers between devices, local(): point_grad = lax.psum(point_terms, 'row')  20.7 us
    dot_general x2, matrix products, local(): mixed = mixed + jnp.dot(points, weights.T, precision=hp)  4.97 us
    unnamed x14, local copies, waits for them, and re-layouts  4.94 us
    dot_general x2, matrix products, local(): cross = jnp.dot(scaled.T, points, precision=hp)  4.88 us
    dot_general x2, matrix products, local(): weights = kernel * jnp.dot(slab_probe.T, probes, precision=hp)  4.77 us
  transfers between devices with their start and end apart: 2, of which 2 were waited for; matrix products, arithmetic and copies ran while one was open for 2% of the time, Pallas kernels for 0%

commit v1 on v0

v1 whole, which is shorter than its diff:
```python
import functools

import jax
import jax.numpy as jnp
from jax import lax
from jax.experimental import pallas as pl
from jax.experimental.pallas import tpu as pltpu
from jax.sharding import PartitionSpec as P

f32, bf16 = jnp.float32, jnp.bfloat16
VMEM_LIMIT = 40 * 2**20


def split(value, parts):
    terms = []
    for _ in range(parts - 1):
        terms.append(value.astype(bf16))
        value = value - terms[-1].astype(f32)
    return terms + [value.astype(bf16)]


def stacked_rows(values, width):
    at = lax.broadcasted_iota(jnp.int32, (16, width), 0)
    block = jnp.zeros((16, width), f32)
    for place, value in enumerate(values):
        block = jnp.where(at == place, value, block)
    return block.astype(bf16)


def pad_rows(blocks, width):
    depth = sum(block.shape[0] for block in blocks)
    short = -depth % 256
    return jnp.concatenate(blocks + ([jnp.zeros((short, width), bf16)] if short else []), axis=0)


def column_weight(inv_ref, emb):
    inv = inv_ref[...]
    return jnp.broadcast_to(inv * inv, (128, emb)).T[:, :1]


def dot(x, y):
    return jnp.dot(x, y, preferred_element_type=f32)


def slab_kernel(width, slab_hbm, slab_probe_hbm, points_hbm, probes_hbm, inv_hbm, terms_ref, high_ref, low_ref,
                slab_ref, slab_probe_ref, points_ref, probes_ref, inv_ref, left, left_probe, total, sems):
    emb, rows = slab_ref.shape
    count = points_ref.shape[1] // width
    pairs = ((inv_hbm, inv_ref), (slab_hbm, slab_ref), (slab_probe_hbm, slab_probe_ref),
             (points_hbm, points_ref), (probes_hbm, probes_ref))
    copies = [pltpu.make_async_copy(src, dst, sems.at[k]) for k, (src, dst) in enumerate(pairs)]
    for copy in copies:
        copy.start()
    for copy in copies[:3]:
        copy.wait()
    weight = column_weight(inv_ref, emb)
    slab = slab_ref[...]
    scaled = slab * weight
    one = jnp.ones((1, rows), f32)
    self_terms = [v.astype(f32) for v in split(-0.5 * jnp.sum(scaled * slab, axis=0, keepdims=True), 3)]
    s1, s2, s3 = split(scaled, 3)
    left[...] = pad_rows([s1, s1, s2, s1, s2, s3, stacked_rows([one] * 3 + self_terms, rows)], rows).T
    p1, p2, p3 = split(slab_probe_ref[...], 3)
    left_probe[...] = pad_rows([p1, p1, p2, p1, p2, p3], rows).T
    for copy in copies[3:]:
        copy.wait()
    one = jnp.ones((1, width), f32)
    for block in range(count):
        columns = pl.ds(block * width, width)
        points = points_ref[:, columns]
        other_terms = [v.astype(f32) for v in split(-0.5 * jnp.sum(weight * points * points, axis=0, keepdims=True), 3)]
        x1, x2, x3 = split(points, 3)
        right = pad_rows([x1, x2, x1, x3, x2, x1, stacked_rows(other_terms + [one] * 3, width)], width)
        q1, q2, q3 = split(probes_ref[:, columns], 3)
        right_probe = pad_rows([q1, q2, q1, q3, q2, q1], width)
        weights = jnp.exp(dot(left[...], right)) * dot(left_probe[...], right_probe)
        high, low = split(weights, 2)
        high_ref[:, columns] = high
        low_ref[:, columns] = low
        both = jnp.concatenate([x1, x2, stacked_rows([one], width)], axis=0)
        nt = (((1,), (1,)), ((), ()))
        part = lax.dot_general(high, both, nt, preferred_element_type=f32) + lax.dot_general(
            low, both, nt, preferred_element_type=f32
        )
        total[...] = part if block == 0 else total[...] + part
    mixed = total[:, : 2 * emb].T
    row_total = total[:, 2 * emb :].T
    terms_ref[...] = -weight * (slab * row_total[:1] - (mixed[:emb] + mixed[emb:]))


def slab_call(slab, slab_probe, points, probes, inv, width):
    emb, rows = slab.shape
    count = points.shape[1]
    any_space = pl.BlockSpec(memory_space=pl.ANY)
    vmem = pl.BlockSpec(memory_space=pltpu.VMEM)
    shapes = [slab.shape, slab_probe.shape, points.shape, probes.shape, inv.shape]
    return pl.pallas_call(
        functools.partial(slab_kernel, width),
        out_shape=(
            jax.ShapeDtypeStruct((emb, rows), f32),
            jax.ShapeDtypeStruct((rows, count), bf16),
            jax.ShapeDtypeStruct((rows, count), bf16),
        ),
        in_specs=[any_space] * 5,
        out_specs=[vmem] * 3,
        scratch_shapes=[pltpu.VMEM(shape, f32) for shape in shapes]
        + [
            pltpu.VMEM((rows, 512), bf16),
            pltpu.VMEM((rows, 256), bf16),
            pltpu.VMEM((rows, 2 * emb + 16), f32),
            pltpu.SemaphoreType.DMA((5,)),
        ],
        compiler_params=pltpu.CompilerParams(vmem_limit_bytes=VMEM_LIMIT),
        cost_estimate=pl.CostEstimate(flops=9 * 10**9, bytes_accessed=5 * 10**6, transcendentals=rows * count),
        name="slab_terms",
    )(slab, slab_probe, points, probes, inv)


def point_kernel(width, slab_ref, points_ref, inv_ref, high_ref, low_ref, terms_ref):
    emb, rows = slab_ref.shape
    weight = column_weight(inv_ref, emb)
    s1, s2 = split(slab_ref[...], 2)
    left = jnp.concatenate([s1, s2, stacked_rows([jnp.ones((1, rows), f32)], rows)], axis=0)
    for block in range(points_ref.shape[1] // width):
        columns = pl.ds(block * width, width)
        sums = dot(left, high_ref[:, columns]) + dot(left, low_ref[:, columns])
        terms_ref[:, columns] = weight * (
            sums[:emb] + sums[emb : 2 * emb] - points_ref[:, columns] * sums[2 * emb : 2 * emb + 1]
        )


def point_call(slab, points, inv, high, low, width):
    rows, count = high.shape
    vmem = pl.BlockSpec(memory_space=pltpu.VMEM)
    return pl.pallas_call(
        functools.partial(point_kernel, width),
        out_shape=jax.ShapeDtypeStruct(points.shape, f32),
        in_specs=[vmem] * 5,
        out_specs=vmem,
        compiler_params=pltpu.CompilerParams(vmem_limit_bytes=VMEM_LIMIT),
        cost_estimate=pl.CostEstimate(flops=2 * 10**9, bytes_accessed=5 * 10**6, transcendentals=0),
        name="point_terms",
    )(slab, points, inv, high, low)


def sum_over(value, axis, size):
    if size & (size - 1):
        return lax.psum(value, axis)
    step = 1
    while step < size:
        value = value + lax.ppermute(value, axis, [(k, k ^ step) for k in range(size)])
        step *= 2
    return value


def solution(mesh):
    def local(slab_embed, slab_probe, point_embed, point_probe, inv_scale):
        inv = inv_scale.reshape(1, -1)
        width = 512 if point_embed.shape[1] % 512 == 0 else point_embed.shape[1]
        slab_terms, high, low = slab_call(slab_embed, slab_probe, point_embed, point_probe, inv, width)
        point_terms = point_call(slab_embed, point_embed, inv, high, low, width)
        slab_grad = sum_over(slab_terms, "col", mesh.shape["col"])
        point_grad = sum_over(point_terms, "row", mesh.shape["row"])
        return slab_grad, point_grad

    placed = (P(None, "row"), P(None, "row"), P(None, "col"), P(None, "col"), P())
    return jax.shard_map(
        local, mesh=mesh, in_specs=placed, out_specs=(P(None, "row"), P(None, "col")), check_vma=False
    )
```

time: 165 us -> 35.5 us (0.22)
  waiting for transfers between devices: 124 us -> 13.3 us
  matrix products: 17.5 us -> 0 us
  between operations: 14.1 us -> 0.68 us
  starting transfers between devices: 0.26 us -> 10.5 us
  Pallas kernels: 0 us -> 4.8 us
  other arithmetic: 3.75 us -> 1.58 us
    psum x2 -> x0, waiting for transfers between devices: 124 us -> none  [the longest x1 103 us: local(): slab_grad = lax.psum(slab_terms, 'col')]
    dot_general x8 -> x0, matrix products: 17.5 us -> none  [the longest x2 4.97 us: local(): mixed = mixed + jnp.dot(points, weights.T, precision=hp)]
    ppermute x0 -> x5, waiting for transfers between devices: none -> 13.3 us  [sum_over(): lax.ppermute(value, axis, [(k, k ^ step) for k in range(size)])]
    ppermute x0 -> x5, starting transfers between devices: none -> 10.5 us  [sum_over(): lax.ppermute(value, axis, [(k, k ^ step) for k in range(size)])]
    pallas_call x0 -> x2, Pallas kernels: none -> 4.8 us  [the longest x1 3.97 us: slab_call(): pl.pallas_call(functools.partial(slab_kernel, width), out_shape=(jax.Shap...]
    reduce_sum x2 -> x0, other arithmetic: 2.17 us -> none  [the longest x1 1.17 us: local(): other_term = jnp.sum(weight_sq[:, None] * points * points, axis=0)]
  transfers between devices with their start and end apart: 2 -> 5, of which waited for: 2 -> 4; matrix products, arithmetic and copies ran while one was open for 2% -> 2% of each run, Pallas kernels for 0% -> 2%
where the time goes in v1:
time: 35.5 us; the launch traced here: 35.2 us
  waiting for transfers between devices  13.3 us (37%)
  starting transfers between devices  10.5 us (30%)
  Pallas kernels  4.8 us (14%)
  local copies, waits for them, and re-layouts  4.39 us (12%)
  other arithmetic  1.58 us (4%)
  between operations  0.68 us (2%)
    ppermute x5, waiting for transfers between devices, sum_over(): lax.ppermute(value, axis, [(k, k ^ step) for k in range(size)])  13.3 us
    ppermute x5, starting transfers between devices, sum_over(): lax.ppermute(value, axis, [(k, k ^ step) for k in range(size)])  10.5 us
    unnamed x14, local copies, waits for them, and re-layouts  4.39 us
    pallas_call x1, Pallas kernels, slab_call(): pl.pallas_call(functools.partial(slab_kernel, width), out_shape=(jax.Shap...  3.97 us
    add x5, other arithmetic, sum_over(): value + lax.ppermute(value, axis, [(k, k ^ step) for k in range(size)])  1.58 us
    pallas_call x1, Pallas kernels, point_call(): pl.pallas_call(functools.partial(point_kernel, width), out_shape=jax.Shap...  0.83 us
  transfers between devices with their start and end apart: 5, of which 4 were waited for; matrix products, arithmetic and copies ran while one was open for 2% of the time, Pallas kernels for 2%

profile of v1, /device:TPU:0, one launch (start us, length us, event | category | flops | bytes accessed | tf_op | source)
XLA Modules:
  0.0 35.2 jit_solution(8882718005324495551)
XLA Ops:
  0.6 0.0 copy-start
  0.6 1.0 %copy-done = f32[64,2048]{1,0:T(8,128)S(1)} copy-done((f32[64,2048]{1,0:T(8,128)S(1)}, f32[64,2048]{1,0:T(8,128)}, u32[]{:S(2)}) %copy-start) | copy-done | bytes 524312
  1.7 0.0 copy-start.2
  1.7 0.9 %copy-done.2 = f32[32,2048]{1,0:T(8,128)S(1)} copy-done((f32[32,2048]{1,0:T(8,128)S(1)}, f32[32,2048]{1,0:T(8,128)}, u32[]{:S(2)}) %copy-start.2) | copy-done | bytes 262168
  2.6 0.0 copy-start.3
  2.6 0.9 %copy-done.3 = f32[64,512]{1,0:T(8,128)S(1)} copy-done((f32[64,512]{1,0:T(8,128)S(1)}, f32[64,512]{1,0:T(8,128)}, u32[]{:S(2)}) %copy-start.3) | copy-done | bytes 131096
  3.5 0.0 copy-start.4
  3.5 0.8 %copy-done.4 = f32[32,512]{1,0:T(8,128)S(1)} copy-done((f32[32,512]{1,0:T(8,128)S(1)}, f32[32,512]{1,0:T(8,128)}, u32[]{:S(2)}) %copy-start.4) | copy-done | bytes 65560
  4.4 0.0 copy-start.5
  4.4 0.7 %copy-done.5 = f32[64]{0:T(128)S(1)} copy-done((f32[64]{0:T(128)S(1)}, f32[64]{0:T(128)}, u32[]{:S(2)}) %copy-start.5) | copy-done | bytes 280
  5.0 0.0 copy-start.1
  5.0 0.0 copy-start.6
  5.0 4.0 %slab_terms.1 = (f32[64,512]{1,0:T(8,128)S(1)}, bf16[512,2048]{1,0:T(8,128)(2,1)S(1)}, bf16[512,2048]{1,0:T(8,128)(2,1)S(1)}) custom-call(f32[64,512]{1,0:T(8,128)S(1)} %copy-done.3, f32[32,512]{1,0:T(8,128)S(1)} %copy-done.4, f32[64,2048]{1,0:T(8,128)S(1)} %copy-done, f32[32,2048]{1,0:T(8,128)S(1)} %copy-done.2, f32[1,64]{1,0:T(1,128)S(1)} %bitcast.1), custom_call_target="tpu_custom_call" | custom-call | flops 8999999488 | bytes 5000000 | tf_op jit(solution)/shard_map/slab_terms/pallas_call | solution.py:97
  9.0 3.0 %collective-permute-start = (f32[64,512]{1,0:T(8,128)S(1)}, f32[64,512]{1,0:T(8,128)S(1)}, u32[]{:S(2)}, u32[]{:S(2)}) collective-permute-start(f32[64,512]{1,0:T(8,128)S(1)} %get-tuple-element.5), channel_id=1, source_target_pairs={{0,2},{2,0},{4,6},{6,4},{8,10},{10,8},{12,14},{14,12},{16,18},{18,... | collective-permute-start | bytes 393224 | tf_op jit(solution)/shard_map/ppermute | solution.py:151
  12.0 0.0 copy-done.1
  12.0 0.0 copy-done.6
  12.0 0.8 %point_terms.1 = f32[64,2048]{1,0:T(8,128)S(1)} custom-call(f32[64,512]{1,0:T(8,128)S(1)} %copy-done.3, f32[64,2048]{1,0:T(8,128)S(1)} %copy-done.1, f32[1,64]{1,0:T(1,128)S(1)} %bitcast.2, bf16[512,2048]{1,0:T(8,128)(2,1)S(1)} %get-tuple-element.6.high_ref, bf16[512,2048]{1,0:T(8,128)(2,1)S(1)} %get-tuple-element.7.low_ref), custom_call_target="tpu_custom_call" | custom-call | flops 2000000000 | bytes 5000000 | tf_op jit(solution)/shard_map/point_terms/pallas_call | solution.py:135
  12.9 0.1 collective-permute-start.4
  12.9 2.6 %collective-permute-done = f32[64,512]{1,0:T(8,128)S(1)} collective-permute-done((f32[64,512]{1,0:T(8,128)S(1)}, f32[64,512]{1,0:T(8,128)S(1)}, u32[]{:S(2)}, u32[]{:S(2)}) %collective-permute-start) | collective-permute-done | bytes 131104 | tf_op jit(solution)/shard_map/ppermute | solution.py:151
  15.5 1.8 %collective-permute-start.1 = (f32[64,512]{1,0:T(8,128)S(1)}, f32[64,512]{1,0:T(8,128)S(1)}, u32[]{:S(2)}, u32[]{:S(2)}) collective-permute-start(f32[64,512]{1,0:T(8,128)S(1)} %add.15), channel_id=1, source_target_pairs={{0,4},{2,6},{4,0},{6,2},{8,12},{10,14},{12,8},{14,10},{16,20},{18,... | collective-permute-start | bytes 393224 | tf_op jit(solution)/shard_map/ppermute | solution.py:151
  17.4 3.2 %collective-permute-done.1 = f32[64,512]{1,0:T(8,128)S(1)} collective-permute-done((f32[64,512]{1,0:T(8,128)S(1)}, f32[64,512]{1,0:T(8,128)S(1)}, u32[]{:S(2)}, u32[]{:S(2)}) %collective-permute-start.1) | collective-permute-done | bytes 131104 | tf_op jit(solution)/shard_map/ppermute | solution.py:151
  20.6 1.9 %collective-permute-start.2 = (f32[64,512]{1,0:T(8,128)S(1)}, f32[64,512]{1,0:T(8,128)S(1)}, u32[]{:S(2)}, u32[]{:S(2)}) collective-permute-start(f32[64,512]{1,0:T(8,128)S(1)} %add.16), channel_id=1, source_target_pairs={{0,8},{2,10},{4,12},{6,14},{8,0},{10,2},{12,4},{14,6},{16,24},{18,... | collective-permute-start | bytes 393224 | tf_op jit(solution)/shard_map/ppermute | solution.py:151
  22.5 3.1 %collective-permute-done.2 = f32[64,512]{1,0:T(8,128)S(1)} collective-permute-done((f32[64,512]{1,0:T(8,128)S(1)}, f32[64,512]{1,0:T(8,128)S(1)}, u32[]{:S(2)}, u32[]{:S(2)}) %collective-permute-start.2) | collective-permute-done | bytes 131104 | tf_op jit(solution)/shard_map/ppermute | solution.py:151
  25.6 3.7 %collective-permute-start.3 = (f32[64,512]{1,0:T(8,128)S(1)}, f32[64,512]{1,0:T(8,128)S(1)}, u32[]{:S(2)}, u32[]{:S(2)}) collective-permute-start(f32[64,512]{1,0:T(8,128)S(1)} %add.17), channel_id=1, source_target_pairs={{0,16},{2,18},{4,20},{6,22},{8,24},{10,26},{12,28},{14,30},{16,0},... | collective-permute-start | bytes 393224 | tf_op jit(solution)/shard_map/ppermute | solution.py:151
  29.4 4.4 %collective-permute-done.3 = f32[64,512]{1,0:T(8,128)S(1)} collective-permute-done((f32[64,512]{1,0:T(8,128)S(1)}, f32[64,512]{1,0:T(8,128)S(1)}, u32[]{:S(2)}, u32[]{:S(2)}) %collective-permute-start.3) | collective-permute-done | bytes 131104 | tf_op jit(solution)/shard_map/ppermute | solution.py:151
  33.7 0.7 %add.18 = f32[64,512]{1,0:T(8,128)} add(f32[64,512]{1,0:T(8,128)S(1)} %add.17, f32[64,512]{1,0:T(8,128)S(1)} %collective-permute-done.3) | non-fusion elementwise | flops 32768 | bytes 393216 | tf_op jit(solution)/shard_map/add | solution.py:151
  34.4 0.0 collective-permute-done.4
  34.4 0.8 %add.19 = f32[64,2048]{1,0:T(8,128)} add(f32[64,2048]{1,0:T(8,128)S(1)} %point_terms.1, f32[64,2048]{1,0:T(8,128)S(1)} %collective-permute-done.4) | non-fusion elementwise | flops 131072 | bytes 1572864 | tf_op jit(solution)/shard_map/add | solution.py:151
  (3 shorter events, 0.1 us)
Async XLA Ops:
  0.6 1.0 %copy-start = (f32[64,2048]{1,0:T(8,128)S(1)}, f32[64,2048]{1,0:T(8,128)}, u32[]{:S(2)}) copy-start(f32[64,2048]{1,0:T(8,128)} %points_ref.1) | copy-start | bytes 1572868
  1.7 0.9 %copy-start.2 = (f32[32,2048]{1,0:T(8,128)S(1)}, f32[32,2048]{1,0:T(8,128)}, u32[]{:S(2)}) copy-start(f32[32,2048]{1,0:T(8,128)} %probes_hbm.1) | copy-start | bytes 786436
  2.6 0.9 %copy-start.3 = (f32[64,512]{1,0:T(8,128)S(1)}, f32[64,512]{1,0:T(8,128)}, u32[]{:S(2)}) copy-start(f32[64,512]{1,0:T(8,128)} %slab_ref.1) | copy-start | bytes 393220
  3.5 0.8 %copy-start.4 = (f32[32,512]{1,0:T(8,128)S(1)}, f32[32,512]{1,0:T(8,128)}, u32[]{:S(2)}) copy-start(f32[32,512]{1,0:T(8,128)} %slab_probe_hbm.1) | copy-start | bytes 196612
  4.4 0.7 %copy-start.5 = (f32[64]{0:T(128)S(1)}, f32[64]{0:T(128)}, u32[]{:S(2)}) copy-start(f32[64]{0:T(128)} %param.9) | copy-start | bytes 772
  5.0 7.0 %copy-start.1 = (f32[64,2048]{1,0:T(8,128)S(1)}, f32[64,2048]{1,0:T(8,128)}, u32[]{:S(2)}) copy-start(f32[64,2048]{1,0:T(8,128)} %points_ref.1) | copy-start | bytes 1572868
  5.0 7.0 %copy-start.6 = (f32[64]{0:T(128)S(1)}, f32[64]{0:T(128)}, u32[]{:S(2)}) copy-start(f32[64]{0:T(128)} %param.9) | copy-start | bytes 772
  9.0 6.5 %collective-permute-start = (f32[64,512]{1,0:T(8,128)S(1)}, f32[64,512]{1,0:T(8,128)S(1)}, u32[]{:S(2)}, u32[]{:S(2)}) collective-permute-start(f32[64,512]{1,0:T(8,128)S(1)} %get-tuple-element.5), channel_id=1, source_target_pairs={{0,2},{2,0},{4,6},{6,4},{8,10},{10,8},{12,14},{14,12},{16,18},{18,... | collective-permute-start | bytes 393224 | tf_op jit(solution)/shard_map/ppermute | solution.py:151
  12.9 21.5 %collective-permute-start.4 = (f32[64,2048]{1,0:T(8,128)S(1)}, f32[64,2048]{1,0:T(8,128)S(1)}, u32[]{:S(2)}, u32[]{:S(2)}) collective-permute-start(f32[64,2048]{1,0:T(8,128)S(1)} %point_terms.1), channel_id=1, source_target_pairs={{0,1},{1,0},{2,3},{3,2},{4,5},{5,4},{6,7},{7,6},{8,9},{9,8},{10,11... | collective-permute-start | bytes 1572872 | tf_op jit(solution)/shard_map/ppermute | solution.py:151
  15.5 5.0 %collective-permute-start.1 = (f32[64,512]{1,0:T(8,128)S(1)}, f32[64,512]{1,0:T(8,128)S(1)}, u32[]{:S(2)}, u32[]{:S(2)}) collective-permute-start(f32[64,512]{1,0:T(8,128)S(1)} %add.15), channel_id=1, source_target_pairs={{0,4},{2,6},{4,0},{6,2},{8,12},{10,14},{12,8},{14,10},{16,20},{18,... | collective-permute-start | bytes 393224 | tf_op jit(solution)/shard_map/ppermute | solution.py:151
  20.6 5.0 %collective-permute-start.2 = (f32[64,512]{1,0:T(8,128)S(1)}, f32[64,512]{1,0:T(8,128)S(1)}, u32[]{:S(2)}, u32[]{:S(2)}) collective-permute-start(f32[64,512]{1,0:T(8,128)S(1)} %add.16), channel_id=1, source_target_pairs={{0,8},{2,10},{4,12},{6,14},{8,0},{10,2},{12,4},{14,6},{16,24},{18,... | collective-permute-start | bytes 393224 | tf_op jit(solution)/shard_map/ppermute | solution.py:151
  25.6 8.1 %collective-permute-start.3 = (f32[64,512]{1,0:T(8,128)S(1)}, f32[64,512]{1,0:T(8,128)S(1)}, u32[]{:S(2)}, u32[]{:S(2)}) collective-permute-start(f32[64,512]{1,0:T(8,128)S(1)} %add.17), channel_id=1, source_target_pairs={{0,16},{2,18},{4,20},{6,22},{8,24},{10,26},{12,28},{14,30},{16,0},... | collective-permute-start | bytes 393224 | tf_op jit(solution)/shard_map/ppermute | solution.py:151

commit v2 on v1

--- a/solution.py
+++ b/solution.py
@@ -45,13 +45,14 @@
 def slab_kernel(width, slab_hbm, slab_probe_hbm, points_hbm, probes_hbm, inv_hbm, terms_ref, high_ref, low_ref,
                 slab_ref, slab_probe_ref, points_ref, probes_ref, inv_ref, left, left_probe, total, sems):
     emb, rows = slab_ref.shape
-    count = points_ref.shape[1] // width
-    pairs = ((inv_hbm, inv_ref), (slab_hbm, slab_ref), (slab_probe_hbm, slab_probe_ref),
-             (points_hbm, points_ref), (probes_hbm, probes_ref))
-    copies = [pltpu.make_async_copy(src, dst, sems.at[k]) for k, (src, dst) in enumerate(pairs)]
-    for copy in copies:
+    columns = [pl.ds(block * width, width) for block in range(points_ref.shape[1] // width)]
+    pairs = [(inv_hbm, inv_ref), (slab_hbm, slab_ref), (slab_probe_hbm, slab_probe_ref)]
+    for here in columns:
+        pairs += [(points_hbm.at[:, here], points_ref.at[:, here]), (probes_hbm.at[:, here], probes_ref.at[:, here])]
+    arriving = [pltpu.make_async_copy(src, dst, sems.at[k]) for k, (src, dst) in enumerate(pairs)]
+    for copy in arriving:
         copy.start()
-    for copy in copies[:3]:
+    for copy in arriving[:3]:
         copy.wait()
     weight = column_weight(inv_ref, emb)
     slab = slab_ref[...]
@@ -62,21 +63,20 @@
     left[...] = pad_rows([s1, s1, s2, s1, s2, s3, stacked_rows([one] * 3 + self_terms, rows)], rows).T
     p1, p2, p3 = split(slab_probe_ref[...], 3)
     left_probe[...] = pad_rows([p1, p1, p2, p1, p2, p3], rows).T
-    for copy in copies[3:]:
-        copy.wait()
     one = jnp.ones((1, width), f32)
-    for block in range(count):
-        columns = pl.ds(block * width, width)
-        points = points_ref[:, columns]
+    for block, here in enumerate(columns):
+        for copy in arriving[3 + 2 * block : 5 + 2 * block]:
+            copy.wait()
+        points = points_ref[:, here]
         other_terms = [v.astype(f32) for v in split(-0.5 * jnp.sum(weight * points * points, axis=0, keepdims=True), 3)]
         x1, x2, x3 = split(points, 3)
         right = pad_rows([x1, x2, x1, x3, x2, x1, stacked_rows(other_terms + [one] * 3, width)], width)
-        q1, q2, q3 = split(probes_ref[:, columns], 3)
+        q1, q2, q3 = split(probes_ref[:, here], 3)
         right_probe = pad_rows([q1, q2, q1, q3, q2, q1], width)
         weights = jnp.exp(dot(left[...], right)) * dot(left_probe[...], right_probe)
         high, low = split(weights, 2)
-        high_ref[:, columns] = high
-        low_ref[:, columns] = low
+        high_ref[:, here] = high
+        low_ref[:, here] = low
         both = jnp.concatenate([x1, x2, stacked_rows([one], width)], axis=0)
         nt = (((1,), (1,)), ((), ()))
         part = lax.dot_general(high, both, nt, preferred_element_type=f32) + lax.dot_general(
@@ -91,29 +91,23 @@
 def slab_call(slab, slab_probe, points, probes, inv, width):
     emb, rows = slab.shape
     count = points.shape[1]
-    any_space = pl.BlockSpec(memory_space=pl.ANY)
-    vmem = pl.BlockSpec(memory_space=pltpu.VMEM)
-    shapes = [slab.shape, slab_probe.shape, points.shape, probes.shape, inv.shape]
+    operands = [pltpu.with_memory_space_constraint(v, pltpu.HBM) for v in (slab, slab_probe, points, probes, inv)]
     return pl.pallas_call(
         functools.partial(slab_kernel, width),
-        out_shape=(
-            jax.ShapeDtypeStruct((emb, rows), f32),
-            jax.ShapeDtypeStruct((rows, count), bf16),
-            jax.ShapeDtypeStruct((rows, count), bf16),
-        ),
-        in_specs=[any_space] * 5,
-        out_specs=[vmem] * 3,
-        scratch_shapes=[pltpu.VMEM(shape, f32) for shape in shapes]
+        out_shape=(pltpu.VMEM((emb, rows), f32), pltpu.VMEM((rows, count), bf16), pltpu.VMEM((rows, count), bf16)),
+        in_specs=[pl.BlockSpec(memory_space=pltpu.HBM)] * 5,
+        out_specs=[pl.BlockSpec(memory_space=pltpu.VMEM)] * 3,
+        scratch_shapes=[pltpu.VMEM(v.shape, f32) for v in operands]
         + [
             pltpu.VMEM((rows, 512), bf16),
             pltpu.VMEM((rows, 256), bf16),
             pltpu.VMEM((rows, 2 * emb + 16), f32),
-            pltpu.SemaphoreType.DMA((5,)),
+            pltpu.SemaphoreType.DMA((3 + 2 * (count // width),)),
         ],
         compiler_params=pltpu.CompilerParams(vmem_limit_bytes=VMEM_LIMIT),
         cost_estimate=pl.CostEstimate(flops=9 * 10**9, bytes_accessed=5 * 10**6, transcendentals=rows * count),
         name="slab_terms",
-    )(slab, slab_probe, points, probes, inv)
+    )(*operands)
 
 
 def point_kernel(width, slab_ref, points_ref, inv_ref, high_ref, low_ref, terms_ref):
@@ -143,14 +137,16 @@
     )(slab, points, inv, high, low)
 
 
-def sum_over(value, axis, size):
+def sum_over(value, axis, size, beside=None):
     if size & (size - 1):
-        return lax.psum(value, axis)
-    step = 1
-    while step < size:
-        value = value + lax.ppermute(value, axis, [(k, k ^ step) for k in range(size)])
-        step *= 2
-    return value
+        return lax.psum(value, axis), beside
+    steps = [1 << bit for bit in range(size.bit_length() - 1)]
+    for place, step in enumerate(steps):
+        other = lax.ppermute(value, axis, [(k, k ^ step) for k in range(size)])
+        if place == len(steps) - 1 and beside is not None:
+            other, beside = lax.optimization_barrier((other, beside))
+        value = value + other
+    return value, beside
 
 
 def solution(mesh):
@@ -159,8 +155,8 @@
         width = 512 if point_embed.shape[1] % 512 == 0 else point_embed.shape[1]
         slab_terms, high, low = slab_call(slab_embed, slab_probe, point_embed, point_probe, inv, width)
         point_terms = point_call(slab_embed, point_embed, inv, high, low, width)
-        slab_grad = sum_over(slab_terms, "col", mesh.shape["col"])
-        point_grad = sum_over(point_terms, "row", mesh.shape["row"])
+        point_grad, _ = sum_over(point_terms, "row", mesh.shape["row"])
+        slab_grad, point_grad = sum_over(slab_terms, "col", mesh.shape["col"], beside=point_grad)
         return slab_grad, point_grad
 
     placed = (P(None, "row"), P(None, "row"), P(None, "col"), P(None, "col"), P())

time: 35.5 us -> 32.6 us (0.918)
  local copies, waits for them, and re-layouts: 4.39 us -> 0.01 us
  Pallas kernels: 4.8 us -> 7.19 us
  waiting for transfers between devices: 13.3 us -> 12.4 us
    unnamed x14 -> x6, local copies, waits for them, and re-layouts: 4.39 us -> 0.01 us
    pallas_call x1, Pallas kernels: 3.97 us -> 6.36 us  [slab_call(): pl.pallas_call(functools.partial(slab_kernel, width), out_shape=(pltpu.VM...]
    ppermute x5, waiting for transfers between devices: 13.3 us -> 12.4 us  [sum_over(): other = lax.ppermute(value, axis, [(k, k ^ step) for k in range(size)])]
  transfers between devices with their start and end apart: 5 -> 5, of which waited for: 4 -> 4; matrix products, arithmetic and copies ran while one was open for 2% -> 3% of each run, Pallas kernels for 2% -> 3%
where the time goes in v2:
time: 32.6 us; the launch traced here: 32.4 us
  waiting for transfers between devices  12.4 us (38%)
  starting transfers between devices  10.5 us (32%)
  Pallas kernels  7.19 us (22%)
  other arithmetic  1.58 us (5%)
  between operations  0.69 us (2%)
    ppermute x5, waiting for transfers between devices, sum_over(): other = lax.ppermute(value, axis, [(k, k ^ step) for k in range(size)])  12.4 us
    ppermute x5, starting transfers between devices, sum_over(): other = lax.ppermute(value, axis, [(k, k ^ step) for k in range(size)])  10.5 us
    pallas_call x1, Pallas kernels, slab_call(): pl.pallas_call(functools.partial(slab_kernel, width), out_shape=(pltpu.VM...  6.36 us
    add x5, other arithmetic, sum_over(): value = value + other  1.58 us
    pallas_call x1, Pallas kernels, point_call(): pl.pallas_call(functools.partial(point_kernel, width), out_shape=jax.Shap...  0.83 us
  transfers between devices with their start and end apart: 5, of which 4 were waited for; matrix products, arithmetic and copies ran while one was open for 3% of the time, Pallas kernels for 3%

profile of v2, /device:TPU:0, one launch (start us, length us, event | category | flops | bytes accessed | tf_op | source)
XLA Modules:
  0.0 32.4 jit_solution(5462918242798626501)
XLA Ops:
  0.6 0.0 copy-start
  0.6 0.0 copy-start.1
  0.7 0.0 copy-start.2
  0.7 6.4 %slab_terms.1 = (f32[64,512]{1,0:T(8,128)S(1)}, bf16[512,2048]{1,0:T(8,128)(2,1)S(1)}, bf16[512,2048]{1,0:T(8,128)(2,1)S(1)}) custom-call(f32[64,512]{1,0:T(8,128)} %slab_ref.1, f32[32,512]{1,0:T(8,128)} %slab_probe_hbm.1, f32[64,2048]{1,0:T(8,128)} %points_ref.1, f32[32,2048]{1,0:T(8,128)} %probes_hbm.1, f32[1,64]{1,0:T(1,128)} %bitcast.1), custom_call_target="tpu_custom_call" | custom-call | flops 8999999488 | bytes 5000000 | tf_op jit(solution)/shard_map/slab_terms/pallas_call | solution.py:95
  7.0 3.0 %collective-permute-start = (f32[64,512]{1,0:T(8,128)S(1)}, f32[64,512]{1,0:T(8,128)S(1)}, u32[]{:S(2)}, u32[]{:S(2)}) collective-permute-start(f32[64,512]{1,0:T(8,128)S(1)} %get-tuple-element.7), channel_id=1, source_target_pairs={{0,2},{2,0},{4,6},{6,4},{8,10},{10,8},{12,14},{14,12},{16,18},{18,... | collective-permute-start | bytes 393224 | tf_op jit(solution)/shard_map/ppermute | solution.py:145
  10.0 0.0 copy-done
  10.0 0.0 copy-done.1
  10.0 0.0 copy-done.2
  10.1 0.8 %point_terms.1 = f32[64,2048]{1,0:T(8,128)S(1)} custom-call(f32[64,512]{1,0:T(8,128)S(1)} %copy-done.1, f32[64,2048]{1,0:T(8,128)S(1)} %copy-done, f32[1,64]{1,0:T(1,128)S(1)} %bitcast.2, bf16[512,2048]{1,0:T(8,128)(2,1)S(1)} %get-tuple-element.8.high_ref, bf16[512,2048]{1,0:T(8,128)(2,1)S(1)} %get-tuple-element.9.low_ref), custom_call_target="tpu_custom_call" | custom-call | flops 2000000000 | bytes 5000000 | tf_op jit(solution)/shard_map/point_terms/pallas_call | solution.py:129
  10.9 0.1 collective-permute-start.4
  11.0 2.6 %collective-permute-done = f32[64,512]{1,0:T(8,128)S(1)} collective-permute-done((f32[64,512]{1,0:T(8,128)S(1)}, f32[64,512]{1,0:T(8,128)S(1)}, u32[]{:S(2)}, u32[]{:S(2)}) %collective-permute-start) | collective-permute-done | bytes 131104 | tf_op jit(solution)/shard_map/ppermute | solution.py:145
  13.5 1.8 %collective-permute-start.1 = (f32[64,512]{1,0:T(8,128)S(1)}, f32[64,512]{1,0:T(8,128)S(1)}, u32[]{:S(2)}, u32[]{:S(2)}) collective-permute-start(f32[64,512]{1,0:T(8,128)S(1)} %add.15), channel_id=1, source_target_pairs={{0,4},{2,6},{4,0},{6,2},{8,12},{10,14},{12,8},{14,10},{16,20},{18,... | collective-permute-start | bytes 393224 | tf_op jit(solution)/shard_map/ppermute | solution.py:145
  15.4 3.2 %collective-permute-done.1 = f32[64,512]{1,0:T(8,128)S(1)} collective-permute-done((f32[64,512]{1,0:T(8,128)S(1)}, f32[64,512]{1,0:T(8,128)S(1)}, u32[]{:S(2)}, u32[]{:S(2)}) %collective-permute-start.1) | collective-permute-done | bytes 131104 | tf_op jit(solution)/shard_map/ppermute | solution.py:145
  18.6 1.9 %collective-permute-start.2 = (f32[64,512]{1,0:T(8,128)S(1)}, f32[64,512]{1,0:T(8,128)S(1)}, u32[]{:S(2)}, u32[]{:S(2)}) collective-permute-start(f32[64,512]{1,0:T(8,128)S(1)} %add.16), channel_id=1, source_target_pairs={{0,8},{2,10},{4,12},{6,14},{8,0},{10,2},{12,4},{14,6},{16,24},{18,... | collective-permute-start | bytes 393224 | tf_op jit(solution)/shard_map/ppermute | solution.py:145
  20.5 3.1 %collective-permute-done.2 = f32[64,512]{1,0:T(8,128)S(1)} collective-permute-done((f32[64,512]{1,0:T(8,128)S(1)}, f32[64,512]{1,0:T(8,128)S(1)}, u32[]{:S(2)}, u32[]{:S(2)}) %collective-permute-start.2) | collective-permute-done | bytes 131104 | tf_op jit(solution)/shard_map/ppermute | solution.py:145
  23.7 3.7 %collective-permute-start.3 = (f32[64,512]{1,0:T(8,128)S(1)}, f32[64,512]{1,0:T(8,128)S(1)}, u32[]{:S(2)}, u32[]{:S(2)}) collective-permute-start(f32[64,512]{1,0:T(8,128)S(1)} %add.17), channel_id=1, source_target_pairs={{0,16},{2,18},{4,20},{6,22},{8,24},{10,26},{12,28},{14,30},{16,0},... | collective-permute-start | bytes 393224 | tf_op jit(solution)/shard_map/ppermute | solution.py:145
  27.4 0.0 collective-permute-done.4
  27.4 0.8 %add.18 = f32[64,2048]{1,0:T(8,128)} add(f32[64,2048]{1,0:T(8,128)S(1)} %point_terms.1, f32[64,2048]{1,0:T(8,128)S(1)} %collective-permute-done.4) | non-fusion elementwise | flops 131072 | bytes 1572864 | tf_op jit(solution)/shard_map/add | solution.py:148
  28.3 3.5 %collective-permute-done.3 = f32[64,512]{1,0:T(8,128)S(1)} collective-permute-done((f32[64,512]{1,0:T(8,128)S(1)}, f32[64,512]{1,0:T(8,128)S(1)}, u32[]{:S(2)}, u32[]{:S(2)}) %collective-permute-start.3) | collective-permute-done | bytes 131104 | tf_op jit(solution)/shard_map/ppermute | solution.py:145
  31.8 0.7 %add.19 = f32[64,512]{1,0:T(8,128)} add(f32[64,512]{1,0:T(8,128)S(1)} %add.17, f32[64,512]{1,0:T(8,128)S(1)} %collective-permute-done.3) | non-fusion elementwise | flops 32768 | bytes 393216 | tf_op jit(solution)/shard_map/add | solution.py:148
  (3 shorter events, 0.1 us)
Async XLA Ops:
  0.6 9.4 %copy-start = (f32[64,2048]{1,0:T(8,128)S(1)}, f32[64,2048]{1,0:T(8,128)}, u32[]{:S(2)}) copy-start(f32[64,2048]{1,0:T(8,128)} %points_ref.1) | copy-start | bytes 1572868
  0.6 9.4 %copy-start.1 = (f32[64,512]{1,0:T(8,128)S(1)}, f32[64,512]{1,0:T(8,128)}, u32[]{:S(2)}) copy-start(f32[64,512]{1,0:T(8,128)} %slab_ref.1) | copy-start | bytes 393220
  0.7 9.4 %copy-start.2 = (f32[64]{0:T(128)S(1)}, f32[64]{0:T(128)}, u32[]{:S(2)}) copy-start(f32[64]{0:T(128)} %param.9) | copy-start | bytes 772
  7.0 6.5 %collective-permute-start = (f32[64,512]{1,0:T(8,128)S(1)}, f32[64,512]{1,0:T(8,128)S(1)}, u32[]{:S(2)}, u32[]{:S(2)}) collective-permute-start(f32[64,512]{1,0:T(8,128)S(1)} %get-tuple-element.7), channel_id=1, source_target_pairs={{0,2},{2,0},{4,6},{6,4},{8,10},{10,8},{12,14},{14,12},{16,18},{18,... | collective-permute-start | bytes 393224 | tf_op jit(solution)/shard_map/ppermute | solution.py:145
  10.9 16.5 %collective-permute-start.4 = (f32[64,2048]{1,0:T(8,128)S(1)}, f32[64,2048]{1,0:T(8,128)S(1)}, u32[]{:S(2)}, u32[]{:S(2)}) collective-permute-start(f32[64,2048]{1,0:T(8,128)S(1)} %point_terms.1), channel_id=1, source_target_pairs={{0,1},{1,0},{2,3},{3,2},{4,5},{5,4},{6,7},{7,6},{8,9},{9,8},{10,11... | collective-permute-start | bytes 1572872 | tf_op jit(solution)/shard_map/ppermute | solution.py:145
  13.5 5.0 %collective-permute-start.1 = (f32[64,512]{1,0:T(8,128)S(1)}, f32[64,512]{1,0:T(8,128)S(1)}, u32[]{:S(2)}, u32[]{:S(2)}) collective-permute-start(f32[64,512]{1,0:T(8,128)S(1)} %add.15), channel_id=1, source_target_pairs={{0,4},{2,6},{4,0},{6,2},{8,12},{10,14},{12,8},{14,10},{16,20},{18,... | collective-permute-start | bytes 393224 | tf_op jit(solution)/shard_map/ppermute | solution.py:145
  18.6 5.0 %collective-permute-start.2 = (f32[64,512]{1,0:T(8,128)S(1)}, f32[64,512]{1,0:T(8,128)S(1)}, u32[]{:S(2)}, u32[]{:S(2)}) collective-permute-start(f32[64,512]{1,0:T(8,128)S(1)} %add.16), channel_id=1, source_target_pairs={{0,8},{2,10},{4,12},{6,14},{8,0},{10,2},{12,4},{14,6},{16,24},{18,... | collective-permute-start | bytes 393224 | tf_op jit(solution)/shard_map/ppermute | solution.py:145
  23.7 8.1 %collective-permute-start.3 = (f32[64,512]{1,0:T(8,128)S(1)}, f32[64,512]{1,0:T(8,128)S(1)}, u32[]{:S(2)}, u32[]{:S(2)}) collective-permute-start(f32[64,512]{1,0:T(8,128)S(1)} %add.17), channel_id=1, source_target_pairs={{0,16},{2,18},{4,20},{6,22},{8,24},{10,26},{12,28},{14,30},{16,0},... | collective-permute-start | bytes 393224 | tf_op jit(solution)/shard_map/ppermute | solution.py:145

commit v3 on v2

--- a/solution.py
+++ b/solution.py
@@ -47,8 +47,7 @@
     emb, rows = slab_ref.shape
     columns = [pl.ds(block * width, width) for block in range(points_ref.shape[1] // width)]
     pairs = [(inv_hbm, inv_ref), (slab_hbm, slab_ref), (slab_probe_hbm, slab_probe_ref)]
-    for here in columns:
-        pairs += [(points_hbm.at[:, here], points_ref.at[:, here]), (probes_hbm.at[:, here], probes_ref.at[:, here])]
+    pairs += [(points_hbm, points_ref), (probes_hbm, probes_ref)]
     arriving = [pltpu.make_async_copy(src, dst, sems.at[k]) for k, (src, dst) in enumerate(pairs)]
     for copy in arriving:
         copy.start()
@@ -63,10 +62,10 @@
     left[...] = pad_rows([s1, s1, s2, s1, s2, s3, stacked_rows([one] * 3 + self_terms, rows)], rows).T
     p1, p2, p3 = split(slab_probe_ref[...], 3)
     left_probe[...] = pad_rows([p1, p1, p2, p1, p2, p3], rows).T
+    for copy in arriving[3:]:
+        copy.wait()
     one = jnp.ones((1, width), f32)
     for block, here in enumerate(columns):
-        for copy in arriving[3 + 2 * block : 5 + 2 * block]:
-            copy.wait()
         points = points_ref[:, here]
         other_terms = [v.astype(f32) for v in split(-0.5 * jnp.sum(weight * points * points, axis=0, keepdims=True), 3)]
         x1, x2, x3 = split(points, 3)
@@ -102,7 +101,7 @@
             pltpu.VMEM((rows, 512), bf16),
             pltpu.VMEM((rows, 256), bf16),
             pltpu.VMEM((rows, 2 * emb + 16), f32),
-            pltpu.SemaphoreType.DMA((3 + 2 * (count // width),)),
+            pltpu.SemaphoreType.DMA((5,)),
         ],
         compiler_params=pltpu.CompilerParams(vmem_limit_bytes=VMEM_LIMIT),
         cost_estimate=pl.CostEstimate(flops=9 * 10**9, bytes_accessed=5 * 10**6, transcendentals=rows * count),
@@ -149,6 +148,26 @@
     return value, beside
 
 
+def sum_over_columns(value, mesh, beside):
+    size, others = mesh.shape["col"], mesh.shape["row"]
+    if size & (size - 1):
+        return lax.psum(value, "col"), beside
+    bits = [1 << bit for bit in range(size.bit_length() - 1)]
+    even = [bits.pop(len(bits) // 2)] + bits
+    odd = [even[k ^ 1] if k ^ 1 < len(even) else even[k] for k in range(len(even))]
+    for place in range(len(even)):
+        pairs = [
+            (col * others + row, (col ^ (odd if row % 2 else even)[place]) * others + row)
+            for col in range(size)
+            for row in range(others)
+        ]
+        other = lax.ppermute(value, ("col", "row"), pairs)
+        if place == len(even) - 1:
+            other, beside = lax.optimization_barrier((other, beside))
+        value = value + other
+    return value, beside
+
+
 def solution(mesh):
     def local(slab_embed, slab_probe, point_embed, point_probe, inv_scale):
         inv = inv_scale.reshape(1, -1)
@@ -156,7 +175,7 @@
         slab_terms, high, low = slab_call(slab_embed, slab_probe, point_embed, point_probe, inv, width)
         point_terms = point_call(slab_embed, point_embed, inv, high, low, width)
         point_grad, _ = sum_over(point_terms, "row", mesh.shape["row"])
-        slab_grad, point_grad = sum_over(slab_terms, "col", mesh.shape["col"], beside=point_grad)
+        slab_grad, point_grad = sum_over_columns(slab_terms, mesh, point_grad)
         return slab_grad, point_grad
 
     placed = (P(None, "row"), P(None, "row"), P(None, "col"), P(None, "col"), P())

time: 32.6 us -> 28.7 us (0.88)
  waiting for transfers between devices: 12.4 us -> 10.2 us
  Pallas kernels: 7.19 us -> 5.49 us
    ppermute x5 -> x1, waiting for transfers between devices: 12.4 us -> 0.01 us  [sum_over(): other = lax.ppermute(value, axis, [(k, k ^ step) for k in range(size)])]
    ppermute x5 -> x1, starting transfers between devices: 10.5 us -> 0.07 us  [sum_over(): other = lax.ppermute(value, axis, [(k, k ^ step) for k in range(size)])]
    ppermute x0 -> x4, starting transfers between devices: none -> 10.2 us  [sum_over_columns(): other = lax.ppermute(value, ('col', 'row'), pairs)]
    ppermute x0 -> x4, waiting for transfers between devices: none -> 10.2 us  [sum_over_columns(): other = lax.ppermute(value, ('col', 'row'), pairs)]
    pallas_call x1, Pallas kernels: 6.36 us -> 4.66 us  [slab_call(): pl.pallas_call(functools.partial(slab_kernel, width), out_shape=(pltpu.VM...]
    add x5 -> x1, other arithmetic: 1.58 us -> 0.85 us  [sum_over(): value = value + other]
    add x0 -> x4, other arithmetic: none -> 0.73 us  [sum_over_columns(): value = value + other]
where the time goes in v3:
time: 28.7 us; the launch traced here: 28.2 us
  starting transfers between devices  10.3 us (36%)
  waiting for transfers between devices  10.2 us (36%)
  Pallas kernels  5.49 us (19%)
  other arithmetic  1.58 us (6%)
  between operations  0.69 us (2%)
    ppermute x4, starting transfers between devices, sum_over_columns(): other = lax.ppermute(value, ('col', 'row'), pairs)  10.2 us
    ppermute x4, waiting for transfers between devices, sum_over_columns(): other = lax.ppermute(value, ('col', 'row'), pairs)  10.2 us
    pallas_call x1, Pallas kernels, slab_call(): pl.pallas_call(functools.partial(slab_kernel, width), out_shape=(pltpu.VM...  4.66 us
    add x1, other arithmetic, sum_over(): value = value + other  0.85 us
    pallas_call x1, Pallas kernels, point_call(): pl.pallas_call(functools.partial(point_kernel, width), out_shape=jax.Shap...  0.83 us
    add x4, other arithmetic, sum_over_columns(): value = value + other  0.73 us
  transfers between devices with their start and end apart: 5, of which 4 were waited for; matrix products, arithmetic and copies ran while one was open for 3% of the time, Pallas kernels for 3%

profile of v3, /device:TPU:0, one launch (start us, length us, event | category | flops | bytes accessed | tf_op | source)
XLA Modules:
  0.0 28.2 jit_solution(9307531520988334430)
XLA Ops:
  0.6 0.0 copy-start
  0.6 0.0 copy-start.1
  0.7 0.0 copy-start.2
  0.7 4.7 %slab_terms.1 = (f32[64,512]{1,0:T(8,128)S(1)}, bf16[512,2048]{1,0:T(8,128)(2,1)S(1)}, bf16[512,2048]{1,0:T(8,128)(2,1)S(1)}) custom-call(f32[64,512]{1,0:T(8,128)} %slab_ref.1, f32[32,512]{1,0:T(8,128)} %slab_probe_hbm.1, f32[64,2048]{1,0:T(8,128)} %points_ref.1, f32[32,2048]{1,0:T(8,128)} %probes_hbm.1, f32[1,64]{1,0:T(1,128)} %bitcast.1), custom_call_target="tpu_custom_call" | custom-call | flops 8999999488 | bytes 5000000 | tf_op jit(solution)/shard_map/slab_terms/pallas_call | solution.py:94
  5.3 3.1 %collective-permute-start = (f32[64,512]{1,0:T(8,128)S(1)}, f32[64,512]{1,0:T(8,128)S(1)}, u32[]{:S(2)}, u32[]{:S(2)}) collective-permute-start(f32[64,512]{1,0:T(8,128)S(1)} %get-tuple-element.7), channel_id=1, source_target_pairs={{0,8},{1,3},{2,10},{3,1},{4,12},{5,7},{6,14},{7,5},{8,0},{9,11},{1... | collective-permute-start | bytes 393224 | tf_op jit(solution)/shard_map/ppermute | solution.py:164
  8.4 0.0 copy-done
  8.4 0.0 copy-done.1
  8.4 0.0 copy-done.2
  8.4 0.8 %point_terms.1 = f32[64,2048]{1,0:T(8,128)S(1)} custom-call(f32[64,512]{1,0:T(8,128)S(1)} %copy-done.1, f32[64,2048]{1,0:T(8,128)S(1)} %copy-done, f32[1,64]{1,0:T(1,128)S(1)} %bitcast.2, bf16[512,2048]{1,0:T(8,128)(2,1)S(1)} %get-tuple-element.8.high_ref, bf16[512,2048]{1,0:T(8,128)(2,1)S(1)} %get-tuple-element.9.low_ref), custom_call_target="tpu_custom_call" | custom-call | flops 2000000000 | bytes 5000000 | tf_op jit(solution)/shard_map/point_terms/pallas_call | solution.py:128
  9.3 0.1 collective-permute-start.4
  9.3 2.0 %collective-permute-done = f32[64,512]{1,0:T(8,128)S(1)} collective-permute-done((f32[64,512]{1,0:T(8,128)S(1)}, f32[64,512]{1,0:T(8,128)S(1)}, u32[]{:S(2)}, u32[]{:S(2)}) %collective-permute-start) | collective-permute-done | bytes 131104 | tf_op jit(solution)/shard_map/ppermute | solution.py:164
  11.4 2.0 %collective-permute-start.1 = (f32[64,512]{1,0:T(8,128)S(1)}, f32[64,512]{1,0:T(8,128)S(1)}, u32[]{:S(2)}, u32[]{:S(2)}) collective-permute-start(f32[64,512]{1,0:T(8,128)S(1)} %add.15), channel_id=1, source_target_pairs={{0,2},{1,9},{2,0},{3,11},{4,6},{5,13},{6,4},{7,15},{8,10},{9,1},{1... | collective-permute-start | bytes 393224 | tf_op jit(solution)/shard_map/ppermute | solution.py:164
  13.4 3.0 %collective-permute-done.1 = f32[64,512]{1,0:T(8,128)S(1)} collective-permute-done((f32[64,512]{1,0:T(8,128)S(1)}, f32[64,512]{1,0:T(8,128)S(1)}, u32[]{:S(2)}, u32[]{:S(2)}) %collective-permute-start.1) | collective-permute-done | bytes 131104 | tf_op jit(solution)/shard_map/ppermute | solution.py:164
  16.4 2.0 %collective-permute-start.2 = (f32[64,512]{1,0:T(8,128)S(1)}, f32[64,512]{1,0:T(8,128)S(1)}, u32[]{:S(2)}, u32[]{:S(2)}) collective-permute-start(f32[64,512]{1,0:T(8,128)S(1)} %add.16), channel_id=1, source_target_pairs={{0,4},{1,17},{2,6},{3,19},{4,0},{5,21},{6,2},{7,23},{8,12},{9,25},... | collective-permute-start | bytes 393224 | tf_op jit(solution)/shard_map/ppermute | solution.py:164
  18.5 3.0 %collective-permute-done.2 = f32[64,512]{1,0:T(8,128)S(1)} collective-permute-done((f32[64,512]{1,0:T(8,128)S(1)}, f32[64,512]{1,0:T(8,128)S(1)}, u32[]{:S(2)}, u32[]{:S(2)}) %collective-permute-start.2) | collective-permute-done | bytes 131104 | tf_op jit(solution)/shard_map/ppermute | solution.py:164
  21.5 3.1 %collective-permute-start.3 = (f32[64,512]{1,0:T(8,128)S(1)}, f32[64,512]{1,0:T(8,128)S(1)}, u32[]{:S(2)}, u32[]{:S(2)}) collective-permute-start(f32[64,512]{1,0:T(8,128)S(1)} %add.17), channel_id=1, source_target_pairs={{0,16},{1,5},{2,18},{3,7},{4,20},{5,1},{6,22},{7,3},{8,24},{9,13},... | collective-permute-start | bytes 393224 | tf_op jit(solution)/shard_map/ppermute | solution.py:164
  24.6 0.0 collective-permute-done.4
  24.6 0.8 %add.18 = f32[64,2048]{1,0:T(8,128)} add(f32[64,2048]{1,0:T(8,128)S(1)} %point_terms.1, f32[64,2048]{1,0:T(8,128)S(1)} %collective-permute-done.4) | non-fusion elementwise | flops 131072 | bytes 1572864 | tf_op jit(solution)/shard_map/add | solution.py:147
  25.4 2.1 %collective-permute-done.3 = f32[64,512]{1,0:T(8,128)S(1)} collective-permute-done((f32[64,512]{1,0:T(8,128)S(1)}, f32[64,512]{1,0:T(8,128)S(1)}, u32[]{:S(2)}, u32[]{:S(2)}) %collective-permute-start.3) | collective-permute-done | bytes 131104 | tf_op jit(solution)/shard_map/ppermute | solution.py:164
  27.6 0.7 %add.19 = f32[64,512]{1,0:T(8,128)} add(f32[64,512]{1,0:T(8,128)S(1)} %add.17, f32[64,512]{1,0:T(8,128)S(1)} %collective-permute-done.3) | non-fusion elementwise | flops 32768 | bytes 393216 | tf_op jit(solution)/shard_map/add | solution.py:167
  (3 shorter events, 0.1 us)
Async XLA Ops:
  0.6 7.8 %copy-start = (f32[64,2048]{1,0:T(8,128)S(1)}, f32[64,2048]{1,0:T(8,128)}, u32[]{:S(2)}) copy-start(f32[64,2048]{1,0:T(8,128)} %points_ref.1) | copy-start | bytes 1572868
  0.6 7.8 %copy-start.1 = (f32[64,512]{1,0:T(8,128)S(1)}, f32[64,512]{1,0:T(8,128)}, u32[]{:S(2)}) copy-start(f32[64,512]{1,0:T(8,128)} %slab_ref.1) | copy-start | bytes 393220
  0.7 7.8 %copy-start.2 = (f32[64]{0:T(128)S(1)}, f32[64]{0:T(128)}, u32[]{:S(2)}) copy-start(f32[64]{0:T(128)} %param.9) | copy-start | bytes 772
  5.3 6.0 %collective-permute-start = (f32[64,512]{1,0:T(8,128)S(1)}, f32[64,512]{1,0:T(8,128)S(1)}, u32[]{:S(2)}, u32[]{:S(2)}) collective-permute-start(f32[64,512]{1,0:T(8,128)S(1)} %get-tuple-element.7), channel_id=1, source_target_pairs={{0,8},{1,3},{2,10},{3,1},{4,12},{5,7},{6,14},{7,5},{8,0},{9,11},{1... | collective-permute-start | bytes 393224 | tf_op jit(solution)/shard_map/ppermute | solution.py:164
  9.3 15.3 %collective-permute-start.4 = (f32[64,2048]{1,0:T(8,128)S(1)}, f32[64,2048]{1,0:T(8,128)S(1)}, u32[]{:S(2)}, u32[]{:S(2)}) collective-permute-start(f32[64,2048]{1,0:T(8,128)S(1)} %point_terms.1), channel_id=1, source_target_pairs={{0,1},{1,0},{2,3},{3,2},{4,5},{5,4},{6,7},{7,6},{8,9},{9,8},{10,11... | collective-permute-start | bytes 1572872 | tf_op jit(solution)/shard_map/ppermute | solution.py:144
  11.4 5.0 %collective-permute-start.1 = (f32[64,512]{1,0:T(8,128)S(1)}, f32[64,512]{1,0:T(8,128)S(1)}, u32[]{:S(2)}, u32[]{:S(2)}) collective-permute-start(f32[64,512]{1,0:T(8,128)S(1)} %add.15), channel_id=1, source_target_pairs={{0,2},{1,9},{2,0},{3,11},{4,6},{5,13},{6,4},{7,15},{8,10},{9,1},{1... | collective-permute-start | bytes 393224 | tf_op jit(solution)/shard_map/ppermute | solution.py:164
  16.4 5.0 %collective-permute-start.2 = (f32[64,512]{1,0:T(8,128)S(1)}, f32[64,512]{1,0:T(8,128)S(1)}, u32[]{:S(2)}, u32[]{:S(2)}) collective-permute-start(f32[64,512]{1,0:T(8,128)S(1)} %add.16), channel_id=1, source_target_pairs={{0,4},{1,17},{2,6},{3,19},{4,0},{5,21},{6,2},{7,23},{8,12},{9,25},... | collective-permute-start | bytes 393224 | tf_op jit(solution)/shard_map/ppermute | solution.py:164
  21.5 6.1 %collective-permute-start.3 = (f32[64,512]{1,0:T(8,128)S(1)}, f32[64,512]{1,0:T(8,128)S(1)}, u32[]{:S(2)}, u32[]{:S(2)}) collective-permute-start(f32[64,512]{1,0:T(8,128)S(1)} %add.17), channel_id=1, source_target_pairs={{0,16},{1,5},{2,18},{3,7},{4,20},{5,1},{6,22},{7,3},{8,24},{9,13},... | collective-permute-start | bytes 393224 | tf_op jit(solution)/shard_map/ppermute | solution.py:164

commit v4 on v3

--- a/solution.py
+++ b/solution.py
@@ -76,15 +76,15 @@
         high, low = split(weights, 2)
         high_ref[:, here] = high
         low_ref[:, here] = low
-        both = jnp.concatenate([x1, x2, stacked_rows([one], width)], axis=0)
+        both = jnp.concatenate([x1, x2, x3, stacked_rows([one], width)], axis=0)
         nt = (((1,), (1,)), ((), ()))
         part = lax.dot_general(high, both, nt, preferred_element_type=f32) + lax.dot_general(
             low, both, nt, preferred_element_type=f32
         )
         total[...] = part if block == 0 else total[...] + part
-    mixed = total[:, : 2 * emb].T
-    row_total = total[:, 2 * emb :].T
-    terms_ref[...] = -weight * (slab * row_total[:1] - (mixed[:emb] + mixed[emb:]))
+    sums = total[...].T
+    mixed = sums[:emb] + (sums[emb : 2 * emb] + sums[2 * emb : 3 * emb])
+    terms_ref[...] = -weight * (slab * sums[3 * emb : 3 * emb + 1] - mixed)
 
 
 def slab_call(slab, slab_probe, points, probes, inv, width):
@@ -100,7 +100,7 @@
         + [
             pltpu.VMEM((rows, 512), bf16),
             pltpu.VMEM((rows, 256), bf16),
-            pltpu.VMEM((rows, 2 * emb + 16), f32),
+            pltpu.VMEM((rows, 3 * emb + 16), f32),
             pltpu.SemaphoreType.DMA((5,)),
         ],
         compiler_params=pltpu.CompilerParams(vmem_limit_bytes=VMEM_LIMIT),
@@ -112,14 +112,13 @@
 def point_kernel(width, slab_ref, points_ref, inv_ref, high_ref, low_ref, terms_ref):
     emb, rows = slab_ref.shape
     weight = column_weight(inv_ref, emb)
-    s1, s2 = split(slab_ref[...], 2)
-    left = jnp.concatenate([s1, s2, stacked_rows([jnp.ones((1, rows), f32)], rows)], axis=0)
+    s1, s2, s3 = split(slab_ref[...], 3)
+    left = jnp.concatenate([s1, s2, s3, stacked_rows([jnp.ones((1, rows), f32)], rows)], axis=0)
     for block in range(points_ref.shape[1] // width):
         columns = pl.ds(block * width, width)
         sums = dot(left, high_ref[:, columns]) + dot(left, low_ref[:, columns])
-        terms_ref[:, columns] = weight * (
-            sums[:emb] + sums[emb : 2 * emb] - points_ref[:, columns] * sums[2 * emb : 2 * emb + 1]
-        )
+        mixed = sums[:emb] + (sums[emb : 2 * emb] + sums[2 * emb : 3 * emb])
+        terms_ref[:, columns] = weight * (mixed - points_ref[:, columns] * sums[3 * emb : 3 * emb + 1])
 
 
 def point_call(slab, points, inv, high, low, width):
@@ -153,11 +152,13 @@
     if size & (size - 1):
         return lax.psum(value, "col"), beside
     bits = [1 << bit for bit in range(size.bit_length() - 1)]
-    even = [bits.pop(len(bits) // 2)] + bits
+    first = bits.pop(len(bits) // 2)
+    even = [first] + bits
     odd = [even[k ^ 1] if k ^ 1 < len(even) else even[k] for k in range(len(even))]
+    late = even[:-2] + even[:-3:-1] if len(even) > 3 else even
     for place in range(len(even)):
         pairs = [
-            (col * others + row, (col ^ (odd if row % 2 else even)[place]) * others + row)
+            (col * others + row, (col ^ (odd if row % 2 else late if col & first else even)[place]) * others + row)
             for col in range(size)
             for row in range(others)
         ]

time: 28.7 us -> 28.4 us (0.990); the launches traced: 28.2 us -> 28.2 us
  waiting for transfers between devices: 10.2 us -> 9.87 us
  Pallas kernels: 5.49 us -> 5.79 us
    pallas_call x1, Pallas kernels: 0.83 us -> 1.12 us  [point_call(): pl.pallas_call(functools.partial(point_kernel, width), out_shape=jax.Shap...]
  transfers between devices with their start and end apart: 5 -> 5, of which waited for: 4 -> 4; matrix products, arithmetic and copies ran while one was open for 3% -> 3% of each run, Pallas kernels for 3% -> 4%
where the time goes in v4:
time: 28.4 us; the launch traced here: 28.2 us
  starting transfers between devices  10.3 us (36%)
  waiting for transfers between devices  9.87 us (35%)
  Pallas kernels  5.79 us (20%)
  other arithmetic  1.58 us (6%)
  between operations  0.69 us (2%)
    ppermute x4, starting transfers between devices, sum_over_columns(): other = lax.ppermute(value, ('col', 'row'), pairs)  10.2 us
    ppermute x4, waiting for transfers between devices, sum_over_columns(): other = lax.ppermute(value, ('col', 'row'), pairs)  9.86 us
    pallas_call x1, Pallas kernels, slab_call(): pl.pallas_call(functools.partial(slab_kernel, width), out_shape=(pltpu.VM...  4.67 us
    pallas_call x1, Pallas kernels, point_call(): pl.pallas_call(functools.partial(point_kernel, width), out_shape=jax.Shap...  1.12 us
    add x1, other arithmetic, sum_over(): value = value + other  0.85 us
    add x4, other arithmetic, sum_over_columns(): value = value + other  0.73 us
  transfers between devices with their start and end apart: 5, of which 4 were waited for; matrix products, arithmetic and copies ran while one was open for 3% of the time, Pallas kernels for 4%

profile of v4, /device:TPU:0, one launch (start us, length us, event | category | flops | bytes accessed | tf_op | source)
XLA Modules:
  0.0 28.2 jit_solution(2086764122467466848)
XLA Ops:
  0.6 0.0 copy-start
  0.6 0.0 copy-start.1
  0.7 0.0 copy-start.2
  0.7 4.7 %slab_terms.1 = (f32[64,512]{1,0:T(8,128)S(1)}, bf16[512,2048]{1,0:T(8,128)(2,1)S(1)}, bf16[512,2048]{1,0:T(8,128)(2,1)S(1)}) custom-call(f32[64,512]{1,0:T(8,128)} %slab_ref.1, f32[32,512]{1,0:T(8,128)} %slab_probe_hbm.1, f32[64,2048]{1,0:T(8,128)} %points_ref.1, f32[32,2048]{1,0:T(8,128)} %probes_hbm.1, f32[1,64]{1,0:T(1,128)} %bitcast.1), custom_call_target="tpu_custom_call" | custom-call | flops 8999999488 | bytes 5000000 | tf_op jit(solution)/shard_map/slab_terms/pallas_call | solution.py:94
  5.3 3.1 %collective-permute-start = (f32[64,512]{1,0:T(8,128)S(1)}, f32[64,512]{1,0:T(8,128)S(1)}, u32[]{:S(2)}, u32[]{:S(2)}) collective-permute-start(f32[64,512]{1,0:T(8,128)S(1)} %get-tuple-element.7), channel_id=1, source_target_pairs={{0,8},{1,3},{2,10},{3,1},{4,12},{5,7},{6,14},{7,5},{8,0},{9,11},{1... | collective-permute-start | bytes 393224 | tf_op jit(solution)/shard_map/ppermute | solution.py:165
  8.4 0.0 copy-done
  8.4 0.0 copy-done.1
  8.4 0.0 copy-done.2
  8.4 1.1 %point_terms.1 = f32[64,2048]{1,0:T(8,128)S(1)} custom-call(f32[64,512]{1,0:T(8,128)S(1)} %copy-done.1, f32[64,2048]{1,0:T(8,128)S(1)} %copy-done, f32[1,64]{1,0:T(1,128)S(1)} %bitcast.2, bf16[512,2048]{1,0:T(8,128)(2,1)S(1)} %get-tuple-element.8.high_ref, bf16[512,2048]{1,0:T(8,128)(2,1)S(1)} %get-tuple-element.9.low_ref), custom_call_target="tpu_custom_call" | custom-call | flops 2000000000 | bytes 5000000 | tf_op jit(solution)/shard_map/point_terms/pallas_call | solution.py:127
  9.6 0.1 collective-permute-start.4
  9.6 1.7 %collective-permute-done = f32[64,512]{1,0:T(8,128)S(1)} collective-permute-done((f32[64,512]{1,0:T(8,128)S(1)}, f32[64,512]{1,0:T(8,128)S(1)}, u32[]{:S(2)}, u32[]{:S(2)}) %collective-permute-start) | collective-permute-done | bytes 131104 | tf_op jit(solution)/shard_map/ppermute | solution.py:165
  11.4 2.0 %collective-permute-start.1 = (f32[64,512]{1,0:T(8,128)S(1)}, f32[64,512]{1,0:T(8,128)S(1)}, u32[]{:S(2)}, u32[]{:S(2)}) collective-permute-start(f32[64,512]{1,0:T(8,128)S(1)} %add.15), channel_id=1, source_target_pairs={{0,2},{1,9},{2,0},{3,11},{4,6},{5,13},{6,4},{7,15},{8,10},{9,1},{1... | collective-permute-start | bytes 393224 | tf_op jit(solution)/shard_map/ppermute | solution.py:165
  13.4 3.0 %collective-permute-done.1 = f32[64,512]{1,0:T(8,128)S(1)} collective-permute-done((f32[64,512]{1,0:T(8,128)S(1)}, f32[64,512]{1,0:T(8,128)S(1)}, u32[]{:S(2)}, u32[]{:S(2)}) %collective-permute-start.1) | collective-permute-done | bytes 131104 | tf_op jit(solution)/shard_map/ppermute | solution.py:165
  16.4 2.0 %collective-permute-start.2 = (f32[64,512]{1,0:T(8,128)S(1)}, f32[64,512]{1,0:T(8,128)S(1)}, u32[]{:S(2)}, u32[]{:S(2)}) collective-permute-start(f32[64,512]{1,0:T(8,128)S(1)} %add.16), channel_id=1, source_target_pairs={{0,4},{1,17},{2,6},{3,19},{4,0},{5,21},{6,2},{7,23},{8,24},{9,25},... | collective-permute-start | bytes 393224 | tf_op jit(solution)/shard_map/ppermute | solution.py:165
  18.5 3.0 %collective-permute-done.2 = f32[64,512]{1,0:T(8,128)S(1)} collective-permute-done((f32[64,512]{1,0:T(8,128)S(1)}, f32[64,512]{1,0:T(8,128)S(1)}, u32[]{:S(2)}, u32[]{:S(2)}) %collective-permute-start.2) | collective-permute-done | bytes 131104 | tf_op jit(solution)/shard_map/ppermute | solution.py:165
  21.5 3.1 %collective-permute-start.3 = (f32[64,512]{1,0:T(8,128)S(1)}, f32[64,512]{1,0:T(8,128)S(1)}, u32[]{:S(2)}, u32[]{:S(2)}) collective-permute-start(f32[64,512]{1,0:T(8,128)S(1)} %add.17), channel_id=1, source_target_pairs={{0,16},{1,5},{2,18},{3,7},{4,20},{5,1},{6,22},{7,3},{8,12},{9,13},... | collective-permute-start | bytes 393224 | tf_op jit(solution)/shard_map/ppermute | solution.py:165
  24.6 0.0 collective-permute-done.4
  24.6 0.8 %add.18 = f32[64,2048]{1,0:T(8,128)} add(f32[64,2048]{1,0:T(8,128)S(1)} %point_terms.1, f32[64,2048]{1,0:T(8,128)S(1)} %collective-permute-done.4) | non-fusion elementwise | flops 131072 | bytes 1572864 | tf_op jit(solution)/shard_map/add | solution.py:146
  25.5 2.1 %collective-permute-done.3 = f32[64,512]{1,0:T(8,128)S(1)} collective-permute-done((f32[64,512]{1,0:T(8,128)S(1)}, f32[64,512]{1,0:T(8,128)S(1)}, u32[]{:S(2)}, u32[]{:S(2)}) %collective-permute-start.3) | collective-permute-done | bytes 131104 | tf_op jit(solution)/shard_map/ppermute | solution.py:165
  27.6 0.7 %add.19 = f32[64,512]{1,0:T(8,128)} add(f32[64,512]{1,0:T(8,128)S(1)} %add.17, f32[64,512]{1,0:T(8,128)S(1)} %collective-permute-done.3) | non-fusion elementwise | flops 32768 | bytes 393216 | tf_op jit(solution)/shard_map/add | solution.py:168
  (3 shorter events, 0.1 us)
Async XLA Ops:
  0.6 7.8 %copy-start = (f32[64,2048]{1,0:T(8,128)S(1)}, f32[64,2048]{1,0:T(8,128)}, u32[]{:S(2)}) copy-start(f32[64,2048]{1,0:T(8,128)} %points_ref.1) | copy-start | bytes 1572868
  0.6 7.8 %copy-start.1 = (f32[64,512]{1,0:T(8,128)S(1)}, f32[64,512]{1,0:T(8,128)}, u32[]{:S(2)}) copy-start(f32[64,512]{1,0:T(8,128)} %slab_ref.1) | copy-start | bytes 393220
  0.7 7.8 %copy-start.2 = (f32[64]{0:T(128)S(1)}, f32[64]{0:T(128)}, u32[]{:S(2)}) copy-start(f32[64]{0:T(128)} %param.9) | copy-start | bytes 772
  5.3 6.0 %collective-permute-start = (f32[64,512]{1,0:T(8,128)S(1)}, f32[64,512]{1,0:T(8,128)S(1)}, u32[]{:S(2)}, u32[]{:S(2)}) collective-permute-start(f32[64,512]{1,0:T(8,128)S(1)} %get-tuple-element.7), channel_id=1, source_target_pairs={{0,8},{1,3},{2,10},{3,1},{4,12},{5,7},{6,14},{7,5},{8,0},{9,11},{1... | collective-permute-start | bytes 393224 | tf_op jit(solution)/shard_map/ppermute | solution.py:165
  9.6 15.0 %collective-permute-start.4 = (f32[64,2048]{1,0:T(8,128)S(1)}, f32[64,2048]{1,0:T(8,128)S(1)}, u32[]{:S(2)}, u32[]{:S(2)}) collective-permute-start(f32[64,2048]{1,0:T(8,128)S(1)} %point_terms.1), channel_id=1, source_target_pairs={{0,1},{1,0},{2,3},{3,2},{4,5},{5,4},{6,7},{7,6},{8,9},{9,8},{10,11... | collective-permute-start | bytes 1572872 | tf_op jit(solution)/shard_map/ppermute | solution.py:143
  11.4 5.0 %collective-permute-start.1 = (f32[64,512]{1,0:T(8,128)S(1)}, f32[64,512]{1,0:T(8,128)S(1)}, u32[]{:S(2)}, u32[]{:S(2)}) collective-permute-start(f32[64,512]{1,0:T(8,128)S(1)} %add.15), channel_id=1, source_target_pairs={{0,2},{1,9},{2,0},{3,11},{4,6},{5,13},{6,4},{7,15},{8,10},{9,1},{1... | collective-permute-start | bytes 393224 | tf_op jit(solution)/shard_map/ppermute | solution.py:165
  16.4 5.0 %collective-permute-start.2 = (f32[64,512]{1,0:T(8,128)S(1)}, f32[64,512]{1,0:T(8,128)S(1)}, u32[]{:S(2)}, u32[]{:S(2)}) collective-permute-start(f32[64,512]{1,0:T(8,128)S(1)} %add.16), channel_id=1, source_target_pairs={{0,4},{1,17},{2,6},{3,19},{4,0},{5,21},{6,2},{7,23},{8,24},{9,25},... | collective-permute-start | bytes 393224 | tf_op jit(solution)/shard_map/ppermute | solution.py:165
  21.5 6.0 %collective-permute-start.3 = (f32[64,512]{1,0:T(8,128)S(1)}, f32[64,512]{1,0:T(8,128)S(1)}, u32[]{:S(2)}, u32[]{:S(2)}) collective-permute-start(f32[64,512]{1,0:T(8,128)S(1)} %add.17), channel_id=1, source_target_pairs={{0,16},{1,5},{2,18},{3,7},{4,20},{5,1},{6,22},{7,3},{8,12},{9,13},... | collective-permute-start | bytes 393224 | tf_op jit(solution)/shard_map/ppermute | solution.py:165

commit v5 on v4

--- a/solution.py
+++ b/solution.py
@@ -33,9 +33,13 @@
     return jnp.concatenate(blocks + ([jnp.zeros((short, width), bf16)] if short else []), axis=0)
 
 
-def column_weight(inv_ref, emb):
-    inv = inv_ref[...]
-    return jnp.broadcast_to(inv * inv, (128, emb)).T[:, :1]
+def column_scale(inv_ref, emb):
+    return jnp.broadcast_to(inv_ref[...], (128, emb)).T[:, :1]
+
+
+def half_square(terms):
+    value = sum(term.astype(f32) for term in terms)
+    return 0.5 * jnp.sum(value * value, axis=0, keepdims=True)
 
 
 def dot(x, y):
@@ -43,7 +47,7 @@
 
 
 def slab_kernel(width, slab_hbm, slab_probe_hbm, points_hbm, probes_hbm, inv_hbm, terms_ref, high_ref, low_ref,
-                slab_ref, slab_probe_ref, points_ref, probes_ref, inv_ref, left, left_probe, total, sems):
+                slab_ref, points_ref, inv_ref, slab_probe_ref, probes_ref, left, left_probe, total, sems):
     emb, rows = slab_ref.shape
     columns = [pl.ds(block * width, width) for block in range(points_ref.shape[1] // width)]
     pairs = [(inv_hbm, inv_ref), (slab_hbm, slab_ref), (slab_probe_hbm, slab_probe_ref)]
@@ -53,30 +57,27 @@
         copy.start()
     for copy in arriving[:3]:
         copy.wait()
-    weight = column_weight(inv_ref, emb)
-    slab = slab_ref[...]
-    scaled = slab * weight
-    one = jnp.ones((1, rows), f32)
-    self_terms = [v.astype(f32) for v in split(-0.5 * jnp.sum(scaled * slab, axis=0, keepdims=True), 3)]
-    s1, s2, s3 = split(scaled, 3)
-    left[...] = pad_rows([s1, s1, s2, s1, s2, s3, stacked_rows([one] * 3 + self_terms, rows)], rows).T
+    scale = column_scale(inv_ref, emb)
+    slab = slab_ref[...] * scale
+    u1, u2 = split(slab, 2)
+    left[...] = jnp.concatenate([u1, u1, u2, u2], axis=0).T
+    slab_square = jnp.broadcast_to(half_square((u1, u2)), (128, rows)).T[:, :1]
     p1, p2, p3 = split(slab_probe_ref[...], 3)
     left_probe[...] = pad_rows([p1, p1, p2, p1, p2, p3], rows).T
     for copy in arriving[3:]:
         copy.wait()
     one = jnp.ones((1, width), f32)
     for block, here in enumerate(columns):
-        points = points_ref[:, here]
-        other_terms = [v.astype(f32) for v in split(-0.5 * jnp.sum(weight * points * points, axis=0, keepdims=True), 3)]
-        x1, x2, x3 = split(points, 3)
-        right = pad_rows([x1, x2, x1, x3, x2, x1, stacked_rows(other_terms + [one] * 3, width)], width)
+        v1, v2, v3 = split(points_ref[:, here] * scale, 3)
+        right = jnp.concatenate([v1, v2, v1, v2], axis=0)
         q1, q2, q3 = split(probes_ref[:, here], 3)
         right_probe = pad_rows([q1, q2, q1, q3, q2, q1], width)
-        weights = jnp.exp(dot(left[...], right)) * dot(left_probe[...], right_probe)
+        exponent = (dot(left[...], right) - slab_square) - half_square((v1, v2))
+        weights = jnp.exp(exponent) * dot(left_probe[...], right_probe)
         high, low = split(weights, 2)
         high_ref[:, here] = high
         low_ref[:, here] = low
-        both = jnp.concatenate([x1, x2, x3, stacked_rows([one], width)], axis=0)
+        both = jnp.concatenate([v1, v2, v3, stacked_rows([one], width)], axis=0)
         nt = (((1,), (1,)), ((), ()))
         part = lax.dot_general(high, both, nt, preferred_element_type=f32) + lax.dot_general(
             low, both, nt, preferred_element_type=f32
@@ -84,7 +85,7 @@
         total[...] = part if block == 0 else total[...] + part
     sums = total[...].T
     mixed = sums[:emb] + (sums[emb : 2 * emb] + sums[2 * emb : 3 * emb])
-    terms_ref[...] = -weight * (slab * sums[3 * emb : 3 * emb + 1] - mixed)
+    terms_ref[...] = -scale * (slab * sums[3 * emb : 3 * emb + 1] - mixed)
 
 
 def slab_call(slab, slab_probe, points, probes, inv, width):
@@ -93,32 +94,39 @@
     operands = [pltpu.with_memory_space_constraint(v, pltpu.HBM) for v in (slab, slab_probe, points, probes, inv)]
     return pl.pallas_call(
         functools.partial(slab_kernel, width),
-        out_shape=(pltpu.VMEM((emb, rows), f32), pltpu.VMEM((rows, count), bf16), pltpu.VMEM((rows, count), bf16)),
+        out_shape=(
+            pltpu.VMEM((emb, rows), f32),
+            pltpu.VMEM((rows, count), bf16),
+            pltpu.VMEM((rows, count), bf16),
+            pltpu.VMEM(slab.shape, f32),
+            pltpu.VMEM(points.shape, f32),
+            pltpu.VMEM(inv.shape, f32),
+        ),
         in_specs=[pl.BlockSpec(memory_space=pltpu.HBM)] * 5,
-        out_specs=[pl.BlockSpec(memory_space=pltpu.VMEM)] * 3,
-        scratch_shapes=[pltpu.VMEM(v.shape, f32) for v in operands]
+        out_specs=[pl.BlockSpec(memory_space=pltpu.VMEM)] * 6,
+        scratch_shapes=[pltpu.VMEM(v.shape, f32) for v in (slab_probe, probes)]
         + [
-            pltpu.VMEM((rows, 512), bf16),
+            pltpu.VMEM((rows, 4 * emb), bf16),
             pltpu.VMEM((rows, 256), bf16),
             pltpu.VMEM((rows, 3 * emb + 16), f32),
             pltpu.SemaphoreType.DMA((5,)),
         ],
         compiler_params=pltpu.CompilerParams(vmem_limit_bytes=VMEM_LIMIT),
-        cost_estimate=pl.CostEstimate(flops=9 * 10**9, bytes_accessed=5 * 10**6, transcendentals=rows * count),
+        cost_estimate=pl.CostEstimate(flops=7 * 10**9, bytes_accessed=5 * 10**6, transcendentals=rows * count),
         name="slab_terms",
     )(*operands)
 
 
 def point_kernel(width, slab_ref, points_ref, inv_ref, high_ref, low_ref, terms_ref):
     emb, rows = slab_ref.shape
-    weight = column_weight(inv_ref, emb)
-    s1, s2, s3 = split(slab_ref[...], 3)
-    left = jnp.concatenate([s1, s2, s3, stacked_rows([jnp.ones((1, rows), f32)], rows)], axis=0)
+    scale = column_scale(inv_ref, emb)
+    u1, u2, u3 = split(slab_ref[...] * scale, 3)
+    left = jnp.concatenate([u1, u2, u3, stacked_rows([jnp.ones((1, rows), f32)], rows)], axis=0)
     for block in range(points_ref.shape[1] // width):
         columns = pl.ds(block * width, width)
         sums = dot(left, high_ref[:, columns]) + dot(left, low_ref[:, columns])
         mixed = sums[:emb] + (sums[emb : 2 * emb] + sums[2 * emb : 3 * emb])
-        terms_ref[:, columns] = weight * (mixed - points_ref[:, columns] * sums[3 * emb : 3 * emb + 1])
+        terms_ref[:, columns] = scale * (mixed - points_ref[:, columns] * scale * sums[3 * emb : 3 * emb + 1])
 
 
 def point_call(slab, points, inv, high, low, width):
@@ -172,9 +180,9 @@
 def solution(mesh):
     def local(slab_embed, slab_probe, point_embed, point_probe, inv_scale):
         inv = inv_scale.reshape(1, -1)
-        width = 512 if point_embed.shape[1] % 512 == 0 else point_embed.shape[1]
-        slab_terms, high, low = slab_call(slab_embed, slab_probe, point_embed, point_probe, inv, width)
-        point_terms = point_call(slab_embed, point_embed, inv, high, low, width)
+        width = 256 if point_embed.shape[1] % 256 == 0 else point_embed.shape[1]
+        slab_terms, high, low, slab, points, scale = slab_call(slab_embed, slab_probe, point_embed, point_probe, inv, width)
+        point_terms = point_call(slab, points, scale, high, low, width)
         point_grad, _ = sum_over(point_terms, "row", mesh.shape["row"])
         slab_grad, point_grad = sum_over_columns(slab_terms, mesh, point_grad)
         return slab_grad, point_grad

time: 28.4 us -> 27.7 us (0.975)
  Pallas kernels: 5.79 us -> 5.26 us
    pallas_call x1, Pallas kernels: 4.67 us -> 4.06 us  [slab_call(): pl.pallas_call(functools.partial(slab_kernel, width), out_shape=(pltpu.VM...]
where the time goes in v5:
time: 27.7 us; the launch traced here: 27.6 us
  starting transfers between devices  10.3 us (37%)
  waiting for transfers between devices  9.79 us (35%)
  Pallas kernels  5.26 us (19%)
  other arithmetic  1.58 us (6%)
  between operations  0.67 us (2%)
    ppermute x4, starting transfers between devices, sum_over_columns(): other = lax.ppermute(value, ('col', 'row'), pairs)  10.2 us
    ppermute x4, waiting for transfers between devices, sum_over_columns(): other = lax.ppermute(value, ('col', 'row'), pairs)  9.79 us
    pallas_call x1, Pallas kernels, slab_call(): pl.pallas_call(functools.partial(slab_kernel, width), out_shape=(pltpu.VM...  4.06 us
    pallas_call x1, Pallas kernels, point_call(): pl.pallas_call(functools.partial(point_kernel, width), out_shape=jax.Shap...  1.2 us
    add x1, other arithmetic, sum_over(): value = value + other  0.85 us
    add x4, other arithmetic, sum_over_columns(): value = value + other  0.73 us
  transfers between devices with their start and end apart: 5, of which 4 were waited for; matrix products, arithmetic and copies ran while one was open for 3% of the time, Pallas kernels for 4%

profile of v5, /device:TPU:0, one launch (start us, length us, event | category | flops | bytes accessed | tf_op | source)
XLA Modules:
  0.0 27.6 jit_solution(17321575526348052410)
XLA Ops:
  0.6 4.1 %slab_terms.1 = (f32[64,512]{1,0:T(8,128)S(1)}, bf16[512,2048]{1,0:T(8,128)(2,1)S(1)}, bf16[512,2048]{1,0:T(8,128)(2,1)S(1)}, f32[64,512]{1,0:T(8,128)S(1)}, f32...) custom-call(f32[64,512]{1,0:T(8,128)} %slab_hbm.1, f32[32,512]{1,0:T(8,128)} %slab_probe_hbm.1, f32[64,2048]{1,0:T(8,128)} %points_hbm.1, ...), custom_call_target="tpu_custom_call" | custom-call | flops 7000000000 | bytes 5000000 | tf_op jit(solution)/shard_map/slab_terms/pallas_call | solution.py:95
  4.7 3.1 %collective-permute-start = (f32[64,512]{1,0:T(8,128)S(1)}, f32[64,512]{1,0:T(8,128)S(1)}, u32[]{:S(2)}, u32[]{:S(2)}) collective-permute-start(f32[64,512]{1,0:T(8,128)S(1)} %get-tuple-element.10), channel_id=1, source_target_pairs={{0,8},{1,3},{2,10},{3,1},{4,12},{5,7},{6,14},{7,5},{8,0},{9,11},{1... | collective-permute-start | bytes 393224 | tf_op jit(solution)/shard_map/ppermute | solution.py:173
  7.8 1.2 %point_terms.1 = f32[64,2048]{1,0:T(8,128)S(1)} custom-call(f32[64,512]{1,0:T(8,128)S(1)} %get-tuple-element.11.slab_ref, f32[64,2048]{1,0:T(8,128)S(1)} %get-tuple-element.12.points_ref, f32[1,64]{1,0:T(1,128)S(1)} %get-tuple-element.13.inv_ref, bf16[512,2048]{1,0:T(8,128)(2,1)S(1)} %get-tuple-element.14.high_ref, ...), custom_call_target="tpu_custom_call" | custom-call | flops 2000000000 | bytes 5000000 | tf_op jit(solution)/shard_map/point_terms/pallas_call | solution.py:135
  9.0 0.1 collective-permute-start.4
  9.1 1.7 %collective-permute-done = f32[64,512]{1,0:T(8,128)S(1)} collective-permute-done((f32[64,512]{1,0:T(8,128)S(1)}, f32[64,512]{1,0:T(8,128)S(1)}, u32[]{:S(2)}, u32[]{:S(2)}) %collective-permute-start) | collective-permute-done | bytes 131104 | tf_op jit(solution)/shard_map/ppermute | solution.py:173
  10.8 2.0 %collective-permute-start.1 = (f32[64,512]{1,0:T(8,128)S(1)}, f32[64,512]{1,0:T(8,128)S(1)}, u32[]{:S(2)}, u32[]{:S(2)}) collective-permute-start(f32[64,512]{1,0:T(8,128)S(1)} %add.15), channel_id=1, source_target_pairs={{0,2},{1,9},{2,0},{3,11},{4,6},{5,13},{6,4},{7,15},{8,10},{9,1},{1... | collective-permute-start | bytes 393224 | tf_op jit(solution)/shard_map/ppermute | solution.py:173
  12.8 3.0 %collective-permute-done.1 = f32[64,512]{1,0:T(8,128)S(1)} collective-permute-done((f32[64,512]{1,0:T(8,128)S(1)}, f32[64,512]{1,0:T(8,128)S(1)}, u32[]{:S(2)}, u32[]{:S(2)}) %collective-permute-start.1) | collective-permute-done | bytes 131104 | tf_op jit(solution)/shard_map/ppermute | solution.py:173
  15.8 2.0 %collective-permute-start.2 = (f32[64,512]{1,0:T(8,128)S(1)}, f32[64,512]{1,0:T(8,128)S(1)}, u32[]{:S(2)}, u32[]{:S(2)}) collective-permute-start(f32[64,512]{1,0:T(8,128)S(1)} %add.16), channel_id=1, source_target_pairs={{0,4},{1,17},{2,6},{3,19},{4,0},{5,21},{6,2},{7,23},{8,24},{9,25},... | collective-permute-start | bytes 393224 | tf_op jit(solution)/shard_map/ppermute | solution.py:173
  17.8 3.0 %collective-permute-done.2 = f32[64,512]{1,0:T(8,128)S(1)} collective-permute-done((f32[64,512]{1,0:T(8,128)S(1)}, f32[64,512]{1,0:T(8,128)S(1)}, u32[]{:S(2)}, u32[]{:S(2)}) %collective-permute-start.2) | collective-permute-done | bytes 131104 | tf_op jit(solution)/shard_map/ppermute | solution.py:173
  20.9 3.1 %collective-permute-start.3 = (f32[64,512]{1,0:T(8,128)S(1)}, f32[64,512]{1,0:T(8,128)S(1)}, u32[]{:S(2)}, u32[]{:S(2)}) collective-permute-start(f32[64,512]{1,0:T(8,128)S(1)} %add.17), channel_id=1, source_target_pairs={{0,16},{1,5},{2,18},{3,7},{4,20},{5,1},{6,22},{7,3},{8,12},{9,13},... | collective-permute-start | bytes 393224 | tf_op jit(solution)/shard_map/ppermute | solution.py:173
  24.0 0.0 collective-permute-done.4
  24.0 0.8 %add.18 = f32[64,2048]{1,0:T(8,128)} add(f32[64,2048]{1,0:T(8,128)S(1)} %point_terms.1, f32[64,2048]{1,0:T(8,128)S(1)} %collective-permute-done.4) | non-fusion elementwise | flops 131072 | bytes 1572864 | tf_op jit(solution)/shard_map/add | solution.py:154
  24.8 2.1 %collective-permute-done.3 = f32[64,512]{1,0:T(8,128)S(1)} collective-permute-done((f32[64,512]{1,0:T(8,128)S(1)}, f32[64,512]{1,0:T(8,128)S(1)}, u32[]{:S(2)}, u32[]{:S(2)}) %collective-permute-start.3) | collective-permute-done | bytes 131104 | tf_op jit(solution)/shard_map/ppermute | solution.py:173
  26.9 0.7 %add.19 = f32[64,512]{1,0:T(8,128)} add(f32[64,512]{1,0:T(8,128)S(1)} %add.17, f32[64,512]{1,0:T(8,128)S(1)} %collective-permute-done.3) | non-fusion elementwise | flops 32768 | bytes 393216 | tf_op jit(solution)/shard_map/add | solution.py:176
  (3 shorter events, 0.1 us)
Async XLA Ops:
  4.7 6.0 %collective-permute-start = (f32[64,512]{1,0:T(8,128)S(1)}, f32[64,512]{1,0:T(8,128)S(1)}, u32[]{:S(2)}, u32[]{:S(2)}) collective-permute-start(f32[64,512]{1,0:T(8,128)S(1)} %get-tuple-element.10), channel_id=1, source_target_pairs={{0,8},{1,3},{2,10},{3,1},{4,12},{5,7},{6,14},{7,5},{8,0},{9,11},{1... | collective-permute-start | bytes 393224 | tf_op jit(solution)/shard_map/ppermute | solution.py:173
  9.0 15.0 %collective-permute-start.4 = (f32[64,2048]{1,0:T(8,128)S(1)}, f32[64,2048]{1,0:T(8,128)S(1)}, u32[]{:S(2)}, u32[]{:S(2)}) collective-permute-start(f32[64,2048]{1,0:T(8,128)S(1)} %point_terms.1), channel_id=1, source_target_pairs={{0,1},{1,0},{2,3},{3,2},{4,5},{5,4},{6,7},{7,6},{8,9},{9,8},{10,11... | collective-permute-start | bytes 1572872 | tf_op jit(solution)/shard_map/ppermute | solution.py:151
  10.8 5.0 %collective-permute-start.1 = (f32[64,512]{1,0:T(8,128)S(1)}, f32[64,512]{1,0:T(8,128)S(1)}, u32[]{:S(2)}, u32[]{:S(2)}) collective-permute-start(f32[64,512]{1,0:T(8,128)S(1)} %add.15), channel_id=1, source_target_pairs={{0,2},{1,9},{2,0},{3,11},{4,6},{5,13},{6,4},{7,15},{8,10},{9,1},{1... | collective-permute-start | bytes 393224 | tf_op jit(solution)/shard_map/ppermute | solution.py:173
  15.8 5.0 %collective-permute-start.2 = (f32[64,512]{1,0:T(8,128)S(1)}, f32[64,512]{1,0:T(8,128)S(1)}, u32[]{:S(2)}, u32[]{:S(2)}) collective-permute-start(f32[64,512]{1,0:T(8,128)S(1)} %add.16), channel_id=1, source_target_pairs={{0,4},{1,17},{2,6},{3,19},{4,0},{5,21},{6,2},{7,23},{8,24},{9,25},... | collective-permute-start | bytes 393224 | tf_op jit(solution)/shard_map/ppermute | solution.py:173
  20.9 6.0 %collective-permute-start.3 = (f32[64,512]{1,0:T(8,128)S(1)}, f32[64,512]{1,0:T(8,128)S(1)}, u32[]{:S(2)}, u32[]{:S(2)}) collective-permute-start(f32[64,512]{1,0:T(8,128)S(1)} %add.17), channel_id=1, source_target_pairs={{0,16},{1,5},{2,18},{3,7},{4,20},{5,1},{6,22},{7,3},{8,12},{9,13},... | collective-permute-start | bytes 393224 | tf_op jit(solution)/shard_map/ppermute | solution.py:173

commit v6 on v5

--- a/solution.py
+++ b/solution.py
@@ -60,32 +60,35 @@
     scale = column_scale(inv_ref, emb)
     slab = slab_ref[...] * scale
     u1, u2 = split(slab, 2)
-    left[...] = jnp.concatenate([u1, u1, u2, u2], axis=0).T
-    slab_square = jnp.broadcast_to(half_square((u1, u2)), (128, rows)).T[:, :1]
+    left[...] = jnp.concatenate([u1, u1, u2, u2], axis=0)
+    slab_square = half_square((u1, u2))
     p1, p2, p3 = split(slab_probe_ref[...], 3)
-    left_probe[...] = pad_rows([p1, p1, p2, p1, p2, p3], rows).T
+    left_probe[...] = pad_rows([p1, p1, p1, p3, p2, p2], rows)
     for copy in arriving[3:]:
         copy.wait()
     one = jnp.ones((1, width), f32)
     for block, here in enumerate(columns):
-        v1, v2, v3 = split(points_ref[:, here] * scale, 3)
-        right = jnp.concatenate([v1, v2, v1, v2], axis=0)
+        points = points_ref[:, here] * scale
+        v1, v2, v3 = split(points, 3)
+        point_square = jnp.broadcast_to(half_square((v1, v2)), (128, width)).T
+        right = jnp.concatenate([v1, v2], axis=0).T
+        right = jnp.concatenate([right, right], axis=1)
         q1, q2, q3 = split(probes_ref[:, here], 3)
-        right_probe = pad_rows([q1, q2, q1, q3, q2, q1], width)
-        exponent = (dot(left[...], right) - slab_square) - half_square((v1, v2))
-        weights = jnp.exp(exponent) * dot(left_probe[...], right_probe)
+        probe_rows = jnp.concatenate([q1, q2, q3, q1], axis=0).T
+        probe_rows = jnp.concatenate([probe_rows, probe_rows], axis=1)
+        exponent = (dot(right, left[...]) - slab_square) - jnp.concatenate([point_square] * (rows // 128), axis=1)
+        weights = jnp.exp(exponent) * dot(probe_rows, left_probe[...])
         high, low = split(weights, 2)
-        high_ref[:, here] = high
-        low_ref[:, here] = low
-        both = jnp.concatenate([v1, v2, v3, stacked_rows([one], width)], axis=0)
-        nt = (((1,), (1,)), ((), ()))
-        part = lax.dot_general(high, both, nt, preferred_element_type=f32) + lax.dot_general(
-            low, both, nt, preferred_element_type=f32
-        )
-        total[...] = part if block == 0 else total[...] + part
-    sums = total[...].T
-    mixed = sums[:emb] + (sums[emb : 2 * emb] + sums[2 * emb : 3 * emb])
-    terms_ref[...] = -scale * (slab * sums[3 * emb : 3 * emb + 1] - mixed)
+        high_ref[here] = high
+        low_ref[here] = low
+        ones = stacked_rows([one], width)
+        part = dot(jnp.concatenate([v1, v2, ones, v3], axis=0), high)
+        part_low = dot(jnp.concatenate([v1, v2, ones], axis=0), low)
+        both = jnp.concatenate([part[: 2 * emb + 16] + part_low, part[2 * emb + 16 :]], axis=0)
+        total[...] = both if block == 0 else total[...] + both
+    sums = total[...]
+    mixed = sums[:emb] + (sums[emb : 2 * emb] + sums[2 * emb + 16 :])
+    terms_ref[...] = -scale * (slab * sums[2 * emb : 2 * emb + 1] - mixed)
 
 
 def slab_call(slab, slab_probe, points, probes, inv, width):
@@ -96,8 +99,8 @@
         functools.partial(slab_kernel, width),
         out_shape=(
             pltpu.VMEM((emb, rows), f32),
-            pltpu.VMEM((rows, count), bf16),
-            pltpu.VMEM((rows, count), bf16),
+            pltpu.VMEM((count, rows), bf16),
+            pltpu.VMEM((count, rows), bf16),
             pltpu.VMEM(slab.shape, f32),
             pltpu.VMEM(points.shape, f32),
             pltpu.VMEM(inv.shape, f32),
@@ -106,9 +109,9 @@
         out_specs=[pl.BlockSpec(memory_space=pltpu.VMEM)] * 6,
         scratch_shapes=[pltpu.VMEM(v.shape, f32) for v in (slab_probe, probes)]
         + [
-            pltpu.VMEM((rows, 4 * emb), bf16),
-            pltpu.VMEM((rows, 256), bf16),
-            pltpu.VMEM((rows, 3 * emb + 16), f32),
+            pltpu.VMEM((4 * emb, rows), bf16),
+            pltpu.VMEM((256, rows), bf16),
+            pltpu.VMEM((3 * emb + 16, rows), f32),
             pltpu.SemaphoreType.DMA((5,)),
         ],
         compiler_params=pltpu.CompilerParams(vmem_limit_bytes=VMEM_LIMIT),
@@ -124,13 +127,15 @@
     left = jnp.concatenate([u1, u2, u3, stacked_rows([jnp.ones((1, rows), f32)], rows)], axis=0)
     for block in range(points_ref.shape[1] // width):
         columns = pl.ds(block * width, width)
-        sums = dot(left, high_ref[:, columns]) + dot(left, low_ref[:, columns])
+        nt = (((1,), (1,)), ((), ()))
+        sums = lax.dot_general(left, high_ref[columns], nt, preferred_element_type=f32) + lax.dot_general(
+            left, low_ref[columns], nt, preferred_element_type=f32
+        )
         mixed = sums[:emb] + (sums[emb : 2 * emb] + sums[2 * emb : 3 * emb])
         terms_ref[:, columns] = scale * (mixed - points_ref[:, columns] * scale * sums[3 * emb : 3 * emb + 1])
 
 
 def point_call(slab, points, inv, high, low, width):
-    rows, count = high.shape
     vmem = pl.BlockSpec(memory_space=pltpu.VMEM)
     return pl.pallas_call(
         functools.partial(point_kernel, width),
@@ -180,7 +185,7 @@
 def solution(mesh):
     def local(slab_embed, slab_probe, point_embed, point_probe, inv_scale):
         inv = inv_scale.reshape(1, -1)
-        width = 256 if point_embed.shape[1] % 256 == 0 else point_embed.shape[1]
+        width = 1024 if point_embed.shape[1] % 1024 == 0 else point_embed.shape[1]
         slab_terms, high, low, slab, points, scale = slab_call(slab_embed, slab_probe, point_embed, point_probe, inv, width)
         point_terms = point_call(slab, points, scale, high, low, width)
         point_grad, _ = sum_over(point_terms, "row", mesh.shape["row"])

time: 27.7 us -> 27.5 us (level)
  waiting for transfers between devices: 9.79 us -> 9.44 us
    pallas_call x1, Pallas kernels: 1.2 us -> 1.56 us  [point_call(): pl.pallas_call(functools.partial(point_kernel, width), out_shape=jax.Shap...]
    ppermute x4, waiting for transfers between devices: 9.79 us -> 9.44 us  [sum_over_columns(): other = lax.ppermute(value, ('col', 'row'), pairs)]
  transfers between devices with their start and end apart: 5 -> 5, of which waited for: 4 -> 4; matrix products, arithmetic and copies ran while one was open for 3% -> 3% of each run, Pallas kernels for 4% -> 6%
where the time goes in v6:
time: 27.5 us; the launch traced here: 27.3 us
  starting transfers between devices  10.3 us (37%)
  waiting for transfers between devices  9.44 us (34%)
  Pallas kernels  5.37 us (20%)
  other arithmetic  1.58 us (6%)
  between operations  0.67 us (2%)
    ppermute x4, starting transfers between devices, sum_over_columns(): other = lax.ppermute(value, ('col', 'row'), pairs)  10.2 us
    ppermute x4, waiting for transfers between devices, sum_over_columns(): other = lax.ppermute(value, ('col', 'row'), pairs)  9.44 us
    pallas_call x1, Pallas kernels, slab_call(): pl.pallas_call(functools.partial(slab_kernel, width), out_shape=(pltpu.VM...  3.82 us
    pallas_call x1, Pallas kernels, point_call(): pl.pallas_call(functools.partial(point_kernel, width), out_shape=jax.Shap...  1.56 us
    add x1, other arithmetic, sum_over(): value = value + other  0.85 us
    add x4, other arithmetic, sum_over_columns(): value = value + other  0.73 us
  transfers between devices with their start and end apart: 5, of which 4 were waited for; matrix products, arithmetic and copies ran while one was open for 3% of the time, Pallas kernels for 6%

profile of v6, /device:TPU:0, one launch (start us, length us, event | category | flops | bytes accessed | tf_op | source)
XLA Modules:
  0.0 27.3 jit_solution(15508250749842666701)
XLA Ops:
  0.6 3.8 %slab_terms.1 = (f32[64,512]{1,0:T(8,128)S(1)}, bf16[2048,512]{1,0:T(8,128)(2,1)S(1)}, bf16[2048,512]{1,0:T(8,128)(2,1)S(1)}, f32[64,512]{1,0:T(8,128)S(1)}, f32...) custom-call(f32[64,512]{1,0:T(8,128)} %slab_hbm.1, f32[32,512]{1,0:T(8,128)} %slab_probe_hbm.1, f32[64,2048]{1,0:T(8,128)} %points_hbm.1, ...), custom_call_target="tpu_custom_call" | custom-call | flops 7000000000 | bytes 5000000 | tf_op jit(solution)/shard_map/slab_terms/pallas_call | solution.py:98
  4.5 3.1 %collective-permute-start = (f32[64,512]{1,0:T(8,128)S(1)}, f32[64,512]{1,0:T(8,128)S(1)}, u32[]{:S(2)}, u32[]{:S(2)}) collective-permute-start(f32[64,512]{1,0:T(8,128)S(1)} %get-tuple-element.10), channel_id=1, source_target_pairs={{0,8},{1,3},{2,10},{3,1},{4,12},{5,7},{6,14},{7,5},{8,0},{9,11},{1... | collective-permute-start | bytes 393224 | tf_op jit(solution)/shard_map/ppermute | solution.py:178
  7.5 1.6 %point_terms.1 = f32[64,2048]{1,0:T(8,128)S(1)} custom-call(f32[64,512]{1,0:T(8,128)S(1)} %get-tuple-element.11.slab_ref, f32[64,2048]{1,0:T(8,128)S(1)} %get-tuple-element.12.points_ref, f32[1,64]{1,0:T(1,128)S(1)} %get-tuple-element.13.inv_ref, bf16[2048,512]{1,0:T(8,128)(2,1)S(1)} %get-tuple-element.14.high_ref, ...), custom_call_target="tpu_custom_call" | custom-call | flops 2000000000 | bytes 5000000 | tf_op jit(solution)/shard_map/point_terms/pallas_call | solution.py:140
  9.1 0.1 collective-permute-start.4
  9.2 1.3 %collective-permute-done = f32[64,512]{1,0:T(8,128)S(1)} collective-permute-done((f32[64,512]{1,0:T(8,128)S(1)}, f32[64,512]{1,0:T(8,128)S(1)}, u32[]{:S(2)}, u32[]{:S(2)}) %collective-permute-start) | collective-permute-done | bytes 131104 | tf_op jit(solution)/shard_map/ppermute | solution.py:178
  10.5 2.0 %collective-permute-start.1 = (f32[64,512]{1,0:T(8,128)S(1)}, f32[64,512]{1,0:T(8,128)S(1)}, u32[]{:S(2)}, u32[]{:S(2)}) collective-permute-start(f32[64,512]{1,0:T(8,128)S(1)} %add.15), channel_id=1, source_target_pairs={{0,2},{1,9},{2,0},{3,11},{4,6},{5,13},{6,4},{7,15},{8,10},{9,1},{1... | collective-permute-start | bytes 393224 | tf_op jit(solution)/shard_map/ppermute | solution.py:178
  12.5 3.0 %collective-permute-done.1 = f32[64,512]{1,0:T(8,128)S(1)} collective-permute-done((f32[64,512]{1,0:T(8,128)S(1)}, f32[64,512]{1,0:T(8,128)S(1)}, u32[]{:S(2)}, u32[]{:S(2)}) %collective-permute-start.1) | collective-permute-done | bytes 131104 | tf_op jit(solution)/shard_map/ppermute | solution.py:178
  15.6 2.0 %collective-permute-start.2 = (f32[64,512]{1,0:T(8,128)S(1)}, f32[64,512]{1,0:T(8,128)S(1)}, u32[]{:S(2)}, u32[]{:S(2)}) collective-permute-start(f32[64,512]{1,0:T(8,128)S(1)} %add.16), channel_id=1, source_target_pairs={{0,4},{1,17},{2,6},{3,19},{4,0},{5,21},{6,2},{7,23},{8,24},{9,25},... | collective-permute-start | bytes 393224 | tf_op jit(solution)/shard_map/ppermute | solution.py:178
  17.6 3.0 %collective-permute-done.2 = f32[64,512]{1,0:T(8,128)S(1)} collective-permute-done((f32[64,512]{1,0:T(8,128)S(1)}, f32[64,512]{1,0:T(8,128)S(1)}, u32[]{:S(2)}, u32[]{:S(2)}) %collective-permute-start.2) | collective-permute-done | bytes 131104 | tf_op jit(solution)/shard_map/ppermute | solution.py:178
  20.6 3.1 %collective-permute-start.3 = (f32[64,512]{1,0:T(8,128)S(1)}, f32[64,512]{1,0:T(8,128)S(1)}, u32[]{:S(2)}, u32[]{:S(2)}) collective-permute-start(f32[64,512]{1,0:T(8,128)S(1)} %add.17), channel_id=1, source_target_pairs={{0,16},{1,5},{2,18},{3,7},{4,20},{5,1},{6,22},{7,3},{8,12},{9,13},... | collective-permute-start | bytes 393224 | tf_op jit(solution)/shard_map/ppermute | solution.py:178
  23.7 0.0 collective-permute-done.4
  23.7 0.8 %add.18 = f32[64,2048]{1,0:T(8,128)} add(f32[64,2048]{1,0:T(8,128)S(1)} %point_terms.1, f32[64,2048]{1,0:T(8,128)S(1)} %collective-permute-done.4) | non-fusion elementwise | flops 131072 | bytes 1572864 | tf_op jit(solution)/shard_map/add | solution.py:159
  24.6 2.1 %collective-permute-done.3 = f32[64,512]{1,0:T(8,128)S(1)} collective-permute-done((f32[64,512]{1,0:T(8,128)S(1)}, f32[64,512]{1,0:T(8,128)S(1)}, u32[]{:S(2)}, u32[]{:S(2)}) %collective-permute-start.3) | collective-permute-done | bytes 131104 | tf_op jit(solution)/shard_map/ppermute | solution.py:178
  26.7 0.7 %add.19 = f32[64,512]{1,0:T(8,128)} add(f32[64,512]{1,0:T(8,128)S(1)} %add.17, f32[64,512]{1,0:T(8,128)S(1)} %collective-permute-done.3) | non-fusion elementwise | flops 32768 | bytes 393216 | tf_op jit(solution)/shard_map/add | solution.py:181
  (3 shorter events, 0.1 us)
Async XLA Ops:
  4.5 6.0 %collective-permute-start = (f32[64,512]{1,0:T(8,128)S(1)}, f32[64,512]{1,0:T(8,128)S(1)}, u32[]{:S(2)}, u32[]{:S(2)}) collective-permute-start(f32[64,512]{1,0:T(8,128)S(1)} %get-tuple-element.10), channel_id=1, source_target_pairs={{0,8},{1,3},{2,10},{3,1},{4,12},{5,7},{6,14},{7,5},{8,0},{9,11},{1... | collective-permute-start | bytes 393224 | tf_op jit(solution)/shard_map/ppermute | solution.py:178
  9.1 14.6 %collective-permute-start.4 = (f32[64,2048]{1,0:T(8,128)S(1)}, f32[64,2048]{1,0:T(8,128)S(1)}, u32[]{:S(2)}, u32[]{:S(2)}) collective-permute-start(f32[64,2048]{1,0:T(8,128)S(1)} %point_terms.1), channel_id=1, source_target_pairs={{0,1},{1,0},{2,3},{3,2},{4,5},{5,4},{6,7},{7,6},{8,9},{9,8},{10,11... | collective-permute-start | bytes 1572872 | tf_op jit(solution)/shard_map/ppermute | solution.py:156
  10.5 5.0 %collective-permute-start.1 = (f32[64,512]{1,0:T(8,128)S(1)}, f32[64,512]{1,0:T(8,128)S(1)}, u32[]{:S(2)}, u32[]{:S(2)}) collective-permute-start(f32[64,512]{1,0:T(8,128)S(1)} %add.15), channel_id=1, source_target_pairs={{0,2},{1,9},{2,0},{3,11},{4,6},{5,13},{6,4},{7,15},{8,10},{9,1},{1... | collective-permute-start | bytes 393224 | tf_op jit(solution)/shard_map/ppermute | solution.py:178
  15.6 5.0 %collective-permute-start.2 = (f32[64,512]{1,0:T(8,128)S(1)}, f32[64,512]{1,0:T(8,128)S(1)}, u32[]{:S(2)}, u32[]{:S(2)}) collective-permute-start(f32[64,512]{1,0:T(8,128)S(1)} %add.16), channel_id=1, source_target_pairs={{0,4},{1,17},{2,6},{3,19},{4,0},{5,21},{6,2},{7,23},{8,24},{9,25},... | collective-permute-start | bytes 393224 | tf_op jit(solution)/shard_map/ppermute | solution.py:178
  20.6 6.0 %collective-permute-start.3 = (f32[64,512]{1,0:T(8,128)S(1)}, f32[64,512]{1,0:T(8,128)S(1)}, u32[]{:S(2)}, u32[]{:S(2)}) collective-permute-start(f32[64,512]{1,0:T(8,128)S(1)} %add.17), channel_id=1, source_target_pairs={{0,16},{1,5},{2,18},{3,7},{4,20},{5,1},{6,22},{7,3},{8,12},{9,13},... | collective-permute-start | bytes 393224 | tf_op jit(solution)/shard_map/ppermute | solution.py:178

commit v7 on v6

--- a/solution.py
+++ b/solution.py
@@ -81,6 +81,7 @@
         high, low = split(weights, 2)
         high_ref[here] = high
         low_ref[here] = low
+        high, low = high_ref[here], low_ref[here]
         ones = stacked_rows([one], width)
         part = dot(jnp.concatenate([v1, v2, ones, v3], axis=0), high)
         part_low = dot(jnp.concatenate([v1, v2, ones], axis=0), low)
@@ -166,12 +167,13 @@
         return lax.psum(value, "col"), beside
     bits = [1 << bit for bit in range(size.bit_length() - 1)]
     first = bits.pop(len(bits) // 2)
-    even = [first] + bits
-    odd = [even[k ^ 1] if k ^ 1 < len(even) else even[k] for k in range(len(even))]
-    late = even[:-2] + even[:-3:-1] if len(even) > 3 else even
+    even, odd = [first] + bits, bits[:1] + [first] + bits[1:]
+    orders = {0: (even, odd), first: (even, odd)}
+    if len(bits) > 2:
+        orders[first] = [first] + bits[-1:] + bits[:-1], bits[:1] + [first] + bits[-1:] + bits[1:-1]
     for place in range(len(even)):
         pairs = [
-            (col * others + row, (col ^ (odd if row % 2 else late if col & first else even)[place]) * others + row)
+            (col * others + row, (col ^ orders[col & first][row % 2][place]) * others + row)
             for col in range(size)
             for row in range(others)
         ]

time: 27.5 us -> 27.4 us (level)
  no operation moved by 1% of the time
where the time goes in v7:
time: 27.4 us; the launch traced here: 27.3 us
  starting transfers between devices  10.3 us (38%)
  waiting for transfers between devices  9.46 us (35%)
  Pallas kernels  5.28 us (19%)
  other arithmetic  1.58 us (6%)
  between operations  0.67 us (2%)
    ppermute x4, starting transfers between devices, sum_over_columns(): other = lax.ppermute(value, ('col', 'row'), pairs)  10.2 us
    ppermute x4, waiting for transfers between devices, sum_over_columns(): other = lax.ppermute(value, ('col', 'row'), pairs)  9.46 us
    pallas_call x1, Pallas kernels, slab_call(): pl.pallas_call(functools.partial(slab_kernel, width), out_shape=(pltpu.VM...  3.74 us
    pallas_call x1, Pallas kernels, point_call(): pl.pallas_call(functools.partial(point_kernel, width), out_shape=jax.Shap...  1.54 us
    add x1, other arithmetic, sum_over(): value = value + other  0.85 us
    add x4, other arithmetic, sum_over_columns(): value = value + other  0.73 us
  transfers between devices with their start and end apart: 5, of which 4 were waited for; matrix products, arithmetic and copies ran while one was open for 3% of the time, Pallas kernels for 6%

profile of v7, /device:TPU:0, one launch (start us, length us, event | category | flops | bytes accessed | tf_op | source)
XLA Modules:
  0.0 27.3 jit_solution(1152504076579113925)
XLA Ops:
  0.6 3.7 %slab_terms.1 = (f32[64,512]{1,0:T(8,128)S(1)}, bf16[2048,512]{1,0:T(8,128)(2,1)S(1)}, bf16[2048,512]{1,0:T(8,128)(2,1)S(1)}, f32[64,512]{1,0:T(8,128)S(1)}, f32...) custom-call(f32[64,512]{1,0:T(8,128)} %slab_hbm.1, f32[32,512]{1,0:T(8,128)} %slab_probe_hbm.1, f32[64,2048]{1,0:T(8,128)} %points_hbm.1, ...), custom_call_target="tpu_custom_call" | custom-call | flops 7000000000 | bytes 5000000 | tf_op jit(solution)/shard_map/slab_terms/pallas_call | solution.py:99
  4.4 3.1 %collective-permute-start = (f32[64,512]{1,0:T(8,128)S(1)}, f32[64,512]{1,0:T(8,128)S(1)}, u32[]{:S(2)}, u32[]{:S(2)}) collective-permute-start(f32[64,512]{1,0:T(8,128)S(1)} %get-tuple-element.10), channel_id=1, source_target_pairs={{0,8},{1,3},{2,10},{3,1},{4,12},{5,7},{6,14},{7,5},{8,0},{9,11},{1... | collective-permute-start | bytes 393224 | tf_op jit(solution)/shard_map/ppermute | solution.py:180
  7.5 1.5 %point_terms.1 = f32[64,2048]{1,0:T(8,128)S(1)} custom-call(f32[64,512]{1,0:T(8,128)S(1)} %get-tuple-element.11.slab_ref, f32[64,2048]{1,0:T(8,128)S(1)} %get-tuple-element.12.points_ref, f32[1,64]{1,0:T(1,128)S(1)} %get-tuple-element.13.inv_ref, bf16[2048,512]{1,0:T(8,128)(2,1)S(1)} %get-tuple-element.14.high_ref, ...), custom_call_target="tpu_custom_call" | custom-call | flops 2000000000 | bytes 5000000 | tf_op jit(solution)/shard_map/point_terms/pallas_call | solution.py:141
  9.0 0.1 collective-permute-start.4
  9.1 1.3 %collective-permute-done = f32[64,512]{1,0:T(8,128)S(1)} collective-permute-done((f32[64,512]{1,0:T(8,128)S(1)}, f32[64,512]{1,0:T(8,128)S(1)}, u32[]{:S(2)}, u32[]{:S(2)}) %collective-permute-start) | collective-permute-done | bytes 131104 | tf_op jit(solution)/shard_map/ppermute | solution.py:180
  10.4 2.0 %collective-permute-start.1 = (f32[64,512]{1,0:T(8,128)S(1)}, f32[64,512]{1,0:T(8,128)S(1)}, u32[]{:S(2)}, u32[]{:S(2)}) collective-permute-start(f32[64,512]{1,0:T(8,128)S(1)} %add.15), channel_id=1, source_target_pairs={{0,2},{1,9},{2,0},{3,11},{4,6},{5,13},{6,4},{7,15},{8,24},{9,1},{1... | collective-permute-start | bytes 393224 | tf_op jit(solution)/shard_map/ppermute | solution.py:180
  12.4 3.0 %collective-permute-done.1 = f32[64,512]{1,0:T(8,128)S(1)} collective-permute-done((f32[64,512]{1,0:T(8,128)S(1)}, f32[64,512]{1,0:T(8,128)S(1)}, u32[]{:S(2)}, u32[]{:S(2)}) %collective-permute-start.1) | collective-permute-done | bytes 131104 | tf_op jit(solution)/shard_map/ppermute | solution.py:180
  15.5 2.0 %collective-permute-start.2 = (f32[64,512]{1,0:T(8,128)S(1)}, f32[64,512]{1,0:T(8,128)S(1)}, u32[]{:S(2)}, u32[]{:S(2)}) collective-permute-start(f32[64,512]{1,0:T(8,128)S(1)} %add.16), channel_id=1, source_target_pairs={{0,4},{1,5},{2,6},{3,7},{4,0},{5,1},{6,2},{7,3},{8,10},{9,25},{10,... | collective-permute-start | bytes 393224 | tf_op jit(solution)/shard_map/ppermute | solution.py:180
  17.5 3.0 %collective-permute-done.2 = f32[64,512]{1,0:T(8,128)S(1)} collective-permute-done((f32[64,512]{1,0:T(8,128)S(1)}, f32[64,512]{1,0:T(8,128)S(1)}, u32[]{:S(2)}, u32[]{:S(2)}) %collective-permute-start.2) | collective-permute-done | bytes 131104 | tf_op jit(solution)/shard_map/ppermute | solution.py:180
  20.6 3.1 %collective-permute-start.3 = (f32[64,512]{1,0:T(8,128)S(1)}, f32[64,512]{1,0:T(8,128)S(1)}, u32[]{:S(2)}, u32[]{:S(2)}) collective-permute-start(f32[64,512]{1,0:T(8,128)S(1)} %add.17), channel_id=1, source_target_pairs={{0,16},{1,17},{2,18},{3,19},{4,20},{5,21},{6,22},{7,23},{8,12},{9,... | collective-permute-start | bytes 393224 | tf_op jit(solution)/shard_map/ppermute | solution.py:180
  23.6 0.0 collective-permute-done.4
  23.7 0.8 %add.18 = f32[64,2048]{1,0:T(8,128)} add(f32[64,2048]{1,0:T(8,128)S(1)} %point_terms.1, f32[64,2048]{1,0:T(8,128)S(1)} %collective-permute-done.4) | non-fusion elementwise | flops 131072 | bytes 1572864 | tf_op jit(solution)/shard_map/add | solution.py:160
  24.5 2.1 %collective-permute-done.3 = f32[64,512]{1,0:T(8,128)S(1)} collective-permute-done((f32[64,512]{1,0:T(8,128)S(1)}, f32[64,512]{1,0:T(8,128)S(1)}, u32[]{:S(2)}, u32[]{:S(2)}) %collective-permute-start.3) | collective-permute-done | bytes 131104 | tf_op jit(solution)/shard_map/ppermute | solution.py:180
  26.6 0.7 %add.19 = f32[64,512]{1,0:T(8,128)} add(f32[64,512]{1,0:T(8,128)S(1)} %add.17, f32[64,512]{1,0:T(8,128)S(1)} %collective-permute-done.3) | non-fusion elementwise | flops 32768 | bytes 393216 | tf_op jit(solution)/shard_map/add | solution.py:183
  (3 shorter events, 0.1 us)
Async XLA Ops:
  4.4 6.0 %collective-permute-start = (f32[64,512]{1,0:T(8,128)S(1)}, f32[64,512]{1,0:T(8,128)S(1)}, u32[]{:S(2)}, u32[]{:S(2)}) collective-permute-start(f32[64,512]{1,0:T(8,128)S(1)} %get-tuple-element.10), channel_id=1, source_target_pairs={{0,8},{1,3},{2,10},{3,1},{4,12},{5,7},{6,14},{7,5},{8,0},{9,11},{1... | collective-permute-start | bytes 393224 | tf_op jit(solution)/shard_map/ppermute | solution.py:180
  9.0 14.6 %collective-permute-start.4 = (f32[64,2048]{1,0:T(8,128)S(1)}, f32[64,2048]{1,0:T(8,128)S(1)}, u32[]{:S(2)}, u32[]{:S(2)}) collective-permute-start(f32[64,2048]{1,0:T(8,128)S(1)} %point_terms.1), channel_id=1, source_target_pairs={{0,1},{1,0},{2,3},{3,2},{4,5},{5,4},{6,7},{7,6},{8,9},{9,8},{10,11... | collective-permute-start | bytes 1572872 | tf_op jit(solution)/shard_map/ppermute | solution.py:157
  10.4 5.0 %collective-permute-start.1 = (f32[64,512]{1,0:T(8,128)S(1)}, f32[64,512]{1,0:T(8,128)S(1)}, u32[]{:S(2)}, u32[]{:S(2)}) collective-permute-start(f32[64,512]{1,0:T(8,128)S(1)} %add.15), channel_id=1, source_target_pairs={{0,2},{1,9},{2,0},{3,11},{4,6},{5,13},{6,4},{7,15},{8,24},{9,1},{1... | collective-permute-start | bytes 393224 | tf_op jit(solution)/shard_map/ppermute | solution.py:180
  15.5 5.0 %collective-permute-start.2 = (f32[64,512]{1,0:T(8,128)S(1)}, f32[64,512]{1,0:T(8,128)S(1)}, u32[]{:S(2)}, u32[]{:S(2)}) collective-permute-start(f32[64,512]{1,0:T(8,128)S(1)} %add.16), channel_id=1, source_target_pairs={{0,4},{1,5},{2,6},{3,7},{4,0},{5,1},{6,2},{7,3},{8,10},{9,25},{10,... | collective-permute-start | bytes 393224 | tf_op jit(solution)/shard_map/ppermute | solution.py:180
  20.6 6.0 %collective-permute-start.3 = (f32[64,512]{1,0:T(8,128)S(1)}, f32[64,512]{1,0:T(8,128)S(1)}, u32[]{:S(2)}, u32[]{:S(2)}) collective-permute-start(f32[64,512]{1,0:T(8,128)S(1)} %add.17), channel_id=1, source_target_pairs={{0,16},{1,17},{2,18},{3,19},{4,20},{5,21},{6,22},{7,23},{8,12},{9,... | collective-permute-start | bytes 393224 | tf_op jit(solution)/shard_map/ppermute | solution.py:180

commit v8 on v7

--- a/solution.py
+++ b/solution.py
@@ -76,11 +76,14 @@
         q1, q2, q3 = split(probes_ref[:, here], 3)
         probe_rows = jnp.concatenate([q1, q2, q3, q1], axis=0).T
         probe_rows = jnp.concatenate([probe_rows, probe_rows], axis=1)
-        exponent = (dot(right, left[...]) - slab_square) - jnp.concatenate([point_square] * (rows // 128), axis=1)
-        weights = jnp.exp(exponent) * dot(probe_rows, left_probe[...])
-        high, low = split(weights, 2)
-        high_ref[here] = high
-        low_ref[here] = low
+        for start in range(0, width, 512):
+            some = slice(start, start + 512)
+            exponent = (dot(right[some], left[...]) - slab_square) - jnp.concatenate([point_square[some]] * (rows // 128), axis=1)
+            weights = jnp.exp(exponent) * dot(probe_rows[some], left_probe[...])
+            high, low = split(weights, 2)
+            at = pl.ds(block * width + start, 512)
+            high_ref[at] = high
+            low_ref[at] = low
         high, low = high_ref[here], low_ref[here]
         ones = stacked_rows([one], width)
         part = dot(jnp.concatenate([v1, v2, ones, v3], axis=0), high)
@@ -189,7 +192,7 @@
         inv = inv_scale.reshape(1, -1)
         width = 1024 if point_embed.shape[1] % 1024 == 0 else point_embed.shape[1]
         slab_terms, high, low, slab, points, scale = slab_call(slab_embed, slab_probe, point_embed, point_probe, inv, width)
-        point_terms = point_call(slab, points, scale, high, low, width)
+        point_terms = point_call(slab, points, scale, high, low, width // 2)
         point_grad, _ = sum_over(point_terms, "row", mesh.shape["row"])
         slab_grad, point_grad = sum_over_columns(slab_terms, mesh, point_grad)
         return slab_grad, point_grad

time: 27.4 us -> 27.4 us (level)
  no operation moved by 1% of the time
where the time goes in v8:
time: 27.4 us; the launch traced here: 27.2 us
  starting transfers between devices  10.3 us (38%)
  waiting for transfers between devices  9.45 us (34%)
  Pallas kernels  5.27 us (19%)
  other arithmetic  1.58 us (6%)
  between operations  0.67 us (2%)
    ppermute x4, starting transfers between devices, sum_over_columns(): other = lax.ppermute(value, ('col', 'row'), pairs)  10.2 us
    ppermute x4, waiting for transfers between devices, sum_over_columns(): other = lax.ppermute(value, ('col', 'row'), pairs)  9.45 us
    pallas_call x1, Pallas kernels, slab_call(): pl.pallas_call(functools.partial(slab_kernel, width), out_shape=(pltpu.VM...  3.71 us
    pallas_call x1, Pallas kernels, point_call(): pl.pallas_call(functools.partial(point_kernel, width), out_shape=jax.Shap...  1.56 us
    add x1, other arithmetic, sum_over(): value = value + other  0.85 us
    add x4, other arithmetic, sum_over_columns(): value = value + other  0.73 us
  transfers between devices with their start and end apart: 5, of which 4 were waited for; matrix products, arithmetic and copies ran while one was open for 3% of the time, Pallas kernels for 6%

profile of v8, /device:TPU:0, one launch (start us, length us, event | category | flops | bytes accessed | tf_op | source)
XLA Modules:
  0.0 27.2 jit_solution(829768027305786084)
XLA Ops:
  0.6 3.7 %slab_terms.1 = (f32[64,512]{1,0:T(8,128)S(1)}, bf16[2048,512]{1,0:T(8,128)(2,1)S(1)}, bf16[2048,512]{1,0:T(8,128)(2,1)S(1)}, f32[64,512]{1,0:T(8,128)S(1)}, f32...) custom-call(f32[64,512]{1,0:T(8,128)} %slab_hbm.1, f32[32,512]{1,0:T(8,128)} %slab_probe_hbm.1, f32[64,2048]{1,0:T(8,128)} %points_hbm.1, ...), custom_call_target="tpu_custom_call" | custom-call | flops 7000000000 | bytes 5000000 | tf_op jit(solution)/shard_map/slab_terms/pallas_call | solution.py:102
  4.3 3.1 %collective-permute-start = (f32[64,512]{1,0:T(8,128)S(1)}, f32[64,512]{1,0:T(8,128)S(1)}, u32[]{:S(2)}, u32[]{:S(2)}) collective-permute-start(f32[64,512]{1,0:T(8,128)S(1)} %get-tuple-element.10), channel_id=1, source_target_pairs={{0,8},{1,3},{2,10},{3,1},{4,12},{5,7},{6,14},{7,5},{8,0},{9,11},{1... | collective-permute-start | bytes 393224 | tf_op jit(solution)/shard_map/ppermute | solution.py:183
  7.4 1.6 %point_terms.1 = f32[64,2048]{1,0:T(8,128)S(1)} custom-call(f32[64,512]{1,0:T(8,128)S(1)} %get-tuple-element.11.slab_ref, f32[64,2048]{1,0:T(8,128)S(1)} %get-tuple-element.12.points_ref, f32[1,64]{1,0:T(1,128)S(1)} %get-tuple-element.13.inv_ref, bf16[2048,512]{1,0:T(8,128)(2,1)S(1)} %get-tuple-element.14.high_ref, ...), custom_call_target="tpu_custom_call" | custom-call | flops 2000000000 | bytes 5000000 | tf_op jit(solution)/shard_map/point_terms/pallas_call | solution.py:144
  9.0 0.1 collective-permute-start.4
  9.1 1.3 %collective-permute-done = f32[64,512]{1,0:T(8,128)S(1)} collective-permute-done((f32[64,512]{1,0:T(8,128)S(1)}, f32[64,512]{1,0:T(8,128)S(1)}, u32[]{:S(2)}, u32[]{:S(2)}) %collective-permute-start) | collective-permute-done | bytes 131104 | tf_op jit(solution)/shard_map/ppermute | solution.py:183
  10.4 2.0 %collective-permute-start.1 = (f32[64,512]{1,0:T(8,128)S(1)}, f32[64,512]{1,0:T(8,128)S(1)}, u32[]{:S(2)}, u32[]{:S(2)}) collective-permute-start(f32[64,512]{1,0:T(8,128)S(1)} %add.15), channel_id=1, source_target_pairs={{0,2},{1,9},{2,0},{3,11},{4,6},{5,13},{6,4},{7,15},{8,24},{9,1},{1... | collective-permute-start | bytes 393224 | tf_op jit(solution)/shard_map/ppermute | solution.py:183
  12.4 3.0 %collective-permute-done.1 = f32[64,512]{1,0:T(8,128)S(1)} collective-permute-done((f32[64,512]{1,0:T(8,128)S(1)}, f32[64,512]{1,0:T(8,128)S(1)}, u32[]{:S(2)}, u32[]{:S(2)}) %collective-permute-start.1) | collective-permute-done | bytes 131104 | tf_op jit(solution)/shard_map/ppermute | solution.py:183
  15.5 2.0 %collective-permute-start.2 = (f32[64,512]{1,0:T(8,128)S(1)}, f32[64,512]{1,0:T(8,128)S(1)}, u32[]{:S(2)}, u32[]{:S(2)}) collective-permute-start(f32[64,512]{1,0:T(8,128)S(1)} %add.16), channel_id=1, source_target_pairs={{0,4},{1,5},{2,6},{3,7},{4,0},{5,1},{6,2},{7,3},{8,10},{9,25},{10,... | collective-permute-start | bytes 393224 | tf_op jit(solution)/shard_map/ppermute | solution.py:183
  17.5 3.0 %collective-permute-done.2 = f32[64,512]{1,0:T(8,128)S(1)} collective-permute-done((f32[64,512]{1,0:T(8,128)S(1)}, f32[64,512]{1,0:T(8,128)S(1)}, u32[]{:S(2)}, u32[]{:S(2)}) %collective-permute-start.2) | collective-permute-done | bytes 131104 | tf_op jit(solution)/shard_map/ppermute | solution.py:183
  20.5 3.1 %collective-permute-start.3 = (f32[64,512]{1,0:T(8,128)S(1)}, f32[64,512]{1,0:T(8,128)S(1)}, u32[]{:S(2)}, u32[]{:S(2)}) collective-permute-start(f32[64,512]{1,0:T(8,128)S(1)} %add.17), channel_id=1, source_target_pairs={{0,16},{1,17},{2,18},{3,19},{4,20},{5,21},{6,22},{7,23},{8,12},{9,... | collective-permute-start | bytes 393224 | tf_op jit(solution)/shard_map/ppermute | solution.py:183
  23.6 0.0 collective-permute-done.4
  23.6 0.8 %add.18 = f32[64,2048]{1,0:T(8,128)} add(f32[64,2048]{1,0:T(8,128)S(1)} %point_terms.1, f32[64,2048]{1,0:T(8,128)S(1)} %collective-permute-done.4) | non-fusion elementwise | flops 131072 | bytes 1572864 | tf_op jit(solution)/shard_map/add | solution.py:163
  24.5 2.1 %collective-permute-done.3 = f32[64,512]{1,0:T(8,128)S(1)} collective-permute-done((f32[64,512]{1,0:T(8,128)S(1)}, f32[64,512]{1,0:T(8,128)S(1)}, u32[]{:S(2)}, u32[]{:S(2)}) %collective-permute-start.3) | collective-permute-done | bytes 131104 | tf_op jit(solution)/shard_map/ppermute | solution.py:183
  26.6 0.7 %add.19 = f32[64,512]{1,0:T(8,128)} add(f32[64,512]{1,0:T(8,128)S(1)} %add.17, f32[64,512]{1,0:T(8,128)S(1)} %collective-permute-done.3) | non-fusion elementwise | flops 32768 | bytes 393216 | tf_op jit(solution)/shard_map/add | solution.py:186
  (3 shorter events, 0.1 us)
Async XLA Ops:
  4.3 6.0 %collective-permute-start = (f32[64,512]{1,0:T(8,128)S(1)}, f32[64,512]{1,0:T(8,128)S(1)}, u32[]{:S(2)}, u32[]{:S(2)}) collective-permute-start(f32[64,512]{1,0:T(8,128)S(1)} %get-tuple-element.10), channel_id=1, source_target_pairs={{0,8},{1,3},{2,10},{3,1},{4,12},{5,7},{6,14},{7,5},{8,0},{9,11},{1... | collective-permute-start | bytes 393224 | tf_op jit(solution)/shard_map/ppermute | solution.py:183
  9.0 14.6 %collective-permute-start.4 = (f32[64,2048]{1,0:T(8,128)S(1)}, f32[64,2048]{1,0:T(8,128)S(1)}, u32[]{:S(2)}, u32[]{:S(2)}) collective-permute-start(f32[64,2048]{1,0:T(8,128)S(1)} %point_terms.1), channel_id=1, source_target_pairs={{0,1},{1,0},{2,3},{3,2},{4,5},{5,4},{6,7},{7,6},{8,9},{9,8},{10,11... | collective-permute-start | bytes 1572872 | tf_op jit(solution)/shard_map/ppermute | solution.py:160
  10.4 5.0 %collective-permute-start.1 = (f32[64,512]{1,0:T(8,128)S(1)}, f32[64,512]{1,0:T(8,128)S(1)}, u32[]{:S(2)}, u32[]{:S(2)}) collective-permute-start(f32[64,512]{1,0:T(8,128)S(1)} %add.15), channel_id=1, source_target_pairs={{0,2},{1,9},{2,0},{3,11},{4,6},{5,13},{6,4},{7,15},{8,24},{9,1},{1... | collective-permute-start | bytes 393224 | tf_op jit(solution)/shard_map/ppermute | solution.py:183
  15.5 5.0 %collective-permute-start.2 = (f32[64,512]{1,0:T(8,128)S(1)}, f32[64,512]{1,0:T(8,128)S(1)}, u32[]{:S(2)}, u32[]{:S(2)}) collective-permute-start(f32[64,512]{1,0:T(8,128)S(1)} %add.16), channel_id=1, source_target_pairs={{0,4},{1,5},{2,6},{3,7},{4,0},{5,1},{6,2},{7,3},{8,10},{9,25},{10,... | collective-permute-start | bytes 393224 | tf_op jit(solution)/shard_map/ppermute | solution.py:183
  20.5 6.0 %collective-permute-start.3 = (f32[64,512]{1,0:T(8,128)S(1)}, f32[64,512]{1,0:T(8,128)S(1)}, u32[]{:S(2)}, u32[]{:S(2)}) collective-permute-start(f32[64,512]{1,0:T(8,128)S(1)} %add.17), channel_id=1, source_target_pairs={{0,16},{1,17},{2,18},{3,19},{4,20},{5,21},{6,22},{7,23},{8,12},{9,... | collective-permute-start | bytes 393224 | tf_op jit(solution)/shard_map/ppermute | solution.py:183

commit v9 on v7

--- a/solution.py
+++ b/solution.py
@@ -170,7 +170,7 @@
     even, odd = [first] + bits, bits[:1] + [first] + bits[1:]
     orders = {0: (even, odd), first: (even, odd)}
     if len(bits) > 2:
-        orders[first] = [first] + bits[-1:] + bits[:-1], bits[:1] + [first] + bits[-1:] + bits[1:-1]
+        orders[first] = [first] + bits[-1:] + bits[:-1], odd
     for place in range(len(even)):
         pairs = [
             (col * others + row, (col ^ orders[col & first][row % 2][place]) * others + row)
@@ -189,7 +189,7 @@
         inv = inv_scale.reshape(1, -1)
         width = 1024 if point_embed.shape[1] % 1024 == 0 else point_embed.shape[1]
         slab_terms, high, low, slab, points, scale = slab_call(slab_embed, slab_probe, point_embed, point_probe, inv, width)
-        point_terms = point_call(slab, points, scale, high, low, width)
+        point_terms = point_call(slab, points, scale, high, low, width // 2)
         point_grad, _ = sum_over(point_terms, "row", mesh.shape["row"])
         slab_grad, point_grad = sum_over_columns(slab_terms, mesh, point_grad)
         return slab_grad, point_grad

time: 27.4 us -> 27.4 us (level)
  no operation moved by 1% of the time
where the time goes in v9:
time: 27.4 us; the launch traced here: 27.3 us
  starting transfers between devices  10.3 us (38%)
  waiting for transfers between devices  9.43 us (34%)
  Pallas kernels  5.31 us (19%)
  other arithmetic  1.58 us (6%)
  between operations  0.67 us (2%)
    ppermute x4, starting transfers between devices, sum_over_columns(): other = lax.ppermute(value, ('col', 'row'), pairs)  10.2 us
    ppermute x4, waiting for transfers between devices, sum_over_columns(): other = lax.ppermute(value, ('col', 'row'), pairs)  9.43 us
    pallas_call x1, Pallas kernels, slab_call(): pl.pallas_call(functools.partial(slab_kernel, width), out_shape=(pltpu.VM...  3.74 us
    pallas_call x1, Pallas kernels, point_call(): pl.pallas_call(functools.partial(point_kernel, width), out_shape=jax.Shap...  1.57 us
    add x1, other arithmetic, sum_over(): value = value + other  0.85 us
    add x4, other arithmetic, sum_over_columns(): value = value + other  0.73 us
  transfers between devices with their start and end apart: 5, of which 4 were waited for; matrix products, arithmetic and copies ran while one was open for 3% of the time, Pallas kernels for 6%

profile of v9, /device:TPU:0, one launch (start us, length us, event | category | flops | bytes accessed | tf_op | source)
XLA Modules:
  0.0 27.3 jit_solution(17786052966789816173)
XLA Ops:
  0.6 3.7 %slab_terms.1 = (f32[64,512]{1,0:T(8,128)S(1)}, bf16[2048,512]{1,0:T(8,128)(2,1)S(1)}, bf16[2048,512]{1,0:T(8,128)(2,1)S(1)}, f32[64,512]{1,0:T(8,128)S(1)}, f32...) custom-call(f32[64,512]{1,0:T(8,128)} %slab_hbm.1, f32[32,512]{1,0:T(8,128)} %slab_probe_hbm.1, f32[64,2048]{1,0:T(8,128)} %points_hbm.1, ...), custom_call_target="tpu_custom_call" | custom-call | flops 7000000000 | bytes 5000000 | tf_op jit(solution)/shard_map/slab_terms/pallas_call | solution.py:99
  4.4 3.1 %collective-permute-start = (f32[64,512]{1,0:T(8,128)S(1)}, f32[64,512]{1,0:T(8,128)S(1)}, u32[]{:S(2)}, u32[]{:S(2)}) collective-permute-start(f32[64,512]{1,0:T(8,128)S(1)} %get-tuple-element.10), channel_id=1, source_target_pairs={{0,8},{1,3},{2,10},{3,1},{4,12},{5,7},{6,14},{7,5},{8,0},{9,11},{1... | collective-permute-start | bytes 393224 | tf_op jit(solution)/shard_map/ppermute | solution.py:180
  7.5 1.6 %point_terms.1 = f32[64,2048]{1,0:T(8,128)S(1)} custom-call(f32[64,512]{1,0:T(8,128)S(1)} %get-tuple-element.11.slab_ref, f32[64,2048]{1,0:T(8,128)S(1)} %get-tuple-element.12.points_ref, f32[1,64]{1,0:T(1,128)S(1)} %get-tuple-element.13.inv_ref, bf16[2048,512]{1,0:T(8,128)(2,1)S(1)} %get-tuple-element.14.high_ref, ...), custom_call_target="tpu_custom_call" | custom-call | flops 2000000000 | bytes 5000000 | tf_op jit(solution)/shard_map/point_terms/pallas_call | solution.py:141
  9.0 0.1 collective-permute-start.4
  9.1 1.3 %collective-permute-done = f32[64,512]{1,0:T(8,128)S(1)} collective-permute-done((f32[64,512]{1,0:T(8,128)S(1)}, f32[64,512]{1,0:T(8,128)S(1)}, u32[]{:S(2)}, u32[]{:S(2)}) %collective-permute-start) | collective-permute-done | bytes 131104 | tf_op jit(solution)/shard_map/ppermute | solution.py:180
  10.4 2.0 %collective-permute-start.1 = (f32[64,512]{1,0:T(8,128)S(1)}, f32[64,512]{1,0:T(8,128)S(1)}, u32[]{:S(2)}, u32[]{:S(2)}) collective-permute-start(f32[64,512]{1,0:T(8,128)S(1)} %add.15), channel_id=1, source_target_pairs={{0,2},{1,9},{2,0},{3,11},{4,6},{5,13},{6,4},{7,15},{8,24},{9,1},{1... | collective-permute-start | bytes 393224 | tf_op jit(solution)/shard_map/ppermute | solution.py:180
  12.4 3.0 %collective-permute-done.1 = f32[64,512]{1,0:T(8,128)S(1)} collective-permute-done((f32[64,512]{1,0:T(8,128)S(1)}, f32[64,512]{1,0:T(8,128)S(1)}, u32[]{:S(2)}, u32[]{:S(2)}) %collective-permute-start.1) | collective-permute-done | bytes 131104 | tf_op jit(solution)/shard_map/ppermute | solution.py:180
  15.5 2.0 %collective-permute-start.2 = (f32[64,512]{1,0:T(8,128)S(1)}, f32[64,512]{1,0:T(8,128)S(1)}, u32[]{:S(2)}, u32[]{:S(2)}) collective-permute-start(f32[64,512]{1,0:T(8,128)S(1)} %add.16), channel_id=1, source_target_pairs={{0,4},{1,5},{2,6},{3,7},{4,0},{5,1},{6,2},{7,3},{8,10},{9,13},{10,... | collective-permute-start | bytes 393224 | tf_op jit(solution)/shard_map/ppermute | solution.py:180
  17.5 3.0 %collective-permute-done.2 = f32[64,512]{1,0:T(8,128)S(1)} collective-permute-done((f32[64,512]{1,0:T(8,128)S(1)}, f32[64,512]{1,0:T(8,128)S(1)}, u32[]{:S(2)}, u32[]{:S(2)}) %collective-permute-start.2) | collective-permute-done | bytes 131104 | tf_op jit(solution)/shard_map/ppermute | solution.py:180
  20.6 3.1 %collective-permute-start.3 = (f32[64,512]{1,0:T(8,128)S(1)}, f32[64,512]{1,0:T(8,128)S(1)}, u32[]{:S(2)}, u32[]{:S(2)}) collective-permute-start(f32[64,512]{1,0:T(8,128)S(1)} %add.17), channel_id=1, source_target_pairs={{0,16},{1,17},{2,18},{3,19},{4,20},{5,21},{6,22},{7,23},{8,12},{9,... | collective-permute-start | bytes 393224 | tf_op jit(solution)/shard_map/ppermute | solution.py:180
  23.6 0.0 collective-permute-done.4
  23.7 0.8 %add.18 = f32[64,2048]{1,0:T(8,128)} add(f32[64,2048]{1,0:T(8,128)S(1)} %point_terms.1, f32[64,2048]{1,0:T(8,128)S(1)} %collective-permute-done.4) | non-fusion elementwise | flops 131072 | bytes 1572864 | tf_op jit(solution)/shard_map/add | solution.py:160
  24.5 2.1 %collective-permute-done.3 = f32[64,512]{1,0:T(8,128)S(1)} collective-permute-done((f32[64,512]{1,0:T(8,128)S(1)}, f32[64,512]{1,0:T(8,128)S(1)}, u32[]{:S(2)}, u32[]{:S(2)}) %collective-permute-start.3) | collective-permute-done | bytes 131104 | tf_op jit(solution)/shard_map/ppermute | solution.py:180
  26.6 0.7 %add.19 = f32[64,512]{1,0:T(8,128)} add(f32[64,512]{1,0:T(8,128)S(1)} %add.17, f32[64,512]{1,0:T(8,128)S(1)} %collective-permute-done.3) | non-fusion elementwise | flops 32768 | bytes 393216 | tf_op jit(solution)/shard_map/add | solution.py:183
  (3 shorter events, 0.1 us)
Async XLA Ops:
  4.4 6.0 %collective-permute-start = (f32[64,512]{1,0:T(8,128)S(1)}, f32[64,512]{1,0:T(8,128)S(1)}, u32[]{:S(2)}, u32[]{:S(2)}) collective-permute-start(f32[64,512]{1,0:T(8,128)S(1)} %get-tuple-element.10), channel_id=1, source_target_pairs={{0,8},{1,3},{2,10},{3,1},{4,12},{5,7},{6,14},{7,5},{8,0},{9,11},{1... | collective-permute-start | bytes 393224 | tf_op jit(solution)/shard_map/ppermute | solution.py:180
  9.0 14.6 %collective-permute-start.4 = (f32[64,2048]{1,0:T(8,128)S(1)}, f32[64,2048]{1,0:T(8,128)S(1)}, u32[]{:S(2)}, u32[]{:S(2)}) collective-permute-start(f32[64,2048]{1,0:T(8,128)S(1)} %point_terms.1), channel_id=1, source_target_pairs={{0,1},{1,0},{2,3},{3,2},{4,5},{5,4},{6,7},{7,6},{8,9},{9,8},{10,11... | collective-permute-start | bytes 1572872 | tf_op jit(solution)/shard_map/ppermute | solution.py:157
  10.4 5.0 %collective-permute-start.1 = (f32[64,512]{1,0:T(8,128)S(1)}, f32[64,512]{1,0:T(8,128)S(1)}, u32[]{:S(2)}, u32[]{:S(2)}) collective-permute-start(f32[64,512]{1,0:T(8,128)S(1)} %add.15), channel_id=1, source_target_pairs={{0,2},{1,9},{2,0},{3,11},{4,6},{5,13},{6,4},{7,15},{8,24},{9,1},{1... | collective-permute-start | bytes 393224 | tf_op jit(solution)/shard_map/ppermute | solution.py:180
  15.5 5.0 %collective-permute-start.2 = (f32[64,512]{1,0:T(8,128)S(1)}, f32[64,512]{1,0:T(8,128)S(1)}, u32[]{:S(2)}, u32[]{:S(2)}) collective-permute-start(f32[64,512]{1,0:T(8,128)S(1)} %add.16), channel_id=1, source_target_pairs={{0,4},{1,5},{2,6},{3,7},{4,0},{5,1},{6,2},{7,3},{8,10},{9,13},{10,... | collective-permute-start | bytes 393224 | tf_op jit(solution)/shard_map/ppermute | solution.py:180
  20.6 6.0 %collective-permute-start.3 = (f32[64,512]{1,0:T(8,128)S(1)}, f32[64,512]{1,0:T(8,128)S(1)}, u32[]{:S(2)}, u32[]{:S(2)}) collective-permute-start(f32[64,512]{1,0:T(8,128)S(1)} %add.17), channel_id=1, source_target_pairs={{0,16},{1,17},{2,18},{3,19},{4,20},{5,21},{6,22},{7,23},{8,12},{9,... | collective-permute-start | bytes 393224 | tf_op jit(solution)/shard_map/ppermute | solution.py:180

commit v10 on v8

--- a/solution.py
+++ b/solution.py
@@ -76,12 +76,12 @@
         q1, q2, q3 = split(probes_ref[:, here], 3)
         probe_rows = jnp.concatenate([q1, q2, q3, q1], axis=0).T
         probe_rows = jnp.concatenate([probe_rows, probe_rows], axis=1)
-        for start in range(0, width, 512):
-            some = slice(start, start + 512)
+        for start in range(0, width, 256):
+            some = slice(start, start + 256)
             exponent = (dot(right[some], left[...]) - slab_square) - jnp.concatenate([point_square[some]] * (rows // 128), axis=1)
             weights = jnp.exp(exponent) * dot(probe_rows[some], left_probe[...])
             high, low = split(weights, 2)
-            at = pl.ds(block * width + start, 512)
+            at = pl.ds(block * width + start, 256)
             high_ref[at] = high
             low_ref[at] = low
         high, low = high_ref[here], low_ref[here]
@@ -173,7 +173,7 @@
     even, odd = [first] + bits, bits[:1] + [first] + bits[1:]
     orders = {0: (even, odd), first: (even, odd)}
     if len(bits) > 2:
-        orders[first] = [first] + bits[-1:] + bits[:-1], bits[:1] + [first] + bits[-1:] + bits[1:-1]
+        orders[first] = [first] + bits[-1:] + bits[:-1], odd
     for place in range(len(even)):
         pairs = [
             (col * others + row, (col ^ orders[col & first][row % 2][place]) * others + row)

time: 27.4 us -> 27.4 us (level)
  no operation moved by 1% of the time
where the time goes in v10:
time: 27.4 us; the launch traced here: 27.3 us
  starting transfers between devices  10.3 us (38%)
  waiting for transfers between devices  9.4 us (34%)
  Pallas kernels  5.3 us (19%)
  other arithmetic  1.58 us (6%)
  between operations  0.67 us (2%)
    ppermute x4, starting transfers between devices, sum_over_columns(): other = lax.ppermute(value, ('col', 'row'), pairs)  10.2 us
    ppermute x4, waiting for transfers between devices, sum_over_columns(): other = lax.ppermute(value, ('col', 'row'), pairs)  9.4 us
    pallas_call x1, Pallas kernels, slab_call(): pl.pallas_call(functools.partial(slab_kernel, width), out_shape=(pltpu.VM...  3.74 us
    pallas_call x1, Pallas kernels, point_call(): pl.pallas_call(functools.partial(point_kernel, width), out_shape=jax.Shap...  1.55 us
    add x1, other arithmetic, sum_over(): value = value + other  0.85 us
    add x4, other arithmetic, sum_over_columns(): value = value + other  0.73 us
  transfers between devices with their start and end apart: 5, of which 4 were waited for; matrix products, arithmetic and copies ran while one was open for 3% of the time, Pallas kernels for 6%

profile of v10, /device:TPU:0, one launch (start us, length us, event | category | flops | bytes accessed | tf_op | source)
XLA Modules:
  0.0 27.3 jit_solution(7118242160342961846)
XLA Ops:
  0.6 3.7 %slab_terms.1 = (f32[64,512]{1,0:T(8,128)S(1)}, bf16[2048,512]{1,0:T(8,128)(2,1)S(1)}, bf16[2048,512]{1,0:T(8,128)(2,1)S(1)}, f32[64,512]{1,0:T(8,128)S(1)}, f32...) custom-call(f32[64,512]{1,0:T(8,128)} %slab_hbm.1, f32[32,512]{1,0:T(8,128)} %slab_probe_hbm.1, f32[64,2048]{1,0:T(8,128)} %points_hbm.1, ...), custom_call_target="tpu_custom_call" | custom-call | flops 7000000000 | bytes 5000000 | tf_op jit(solution)/shard_map/slab_terms/pallas_call | solution.py:102
  4.4 3.1 %collective-permute-start = (f32[64,512]{1,0:T(8,128)S(1)}, f32[64,512]{1,0:T(8,128)S(1)}, u32[]{:S(2)}, u32[]{:S(2)}) collective-permute-start(f32[64,512]{1,0:T(8,128)S(1)} %get-tuple-element.10), channel_id=1, source_target_pairs={{0,8},{1,3},{2,10},{3,1},{4,12},{5,7},{6,14},{7,5},{8,0},{9,11},{1... | collective-permute-start | bytes 393224 | tf_op jit(solution)/shard_map/ppermute | solution.py:183
  7.5 1.6 %point_terms.1 = f32[64,2048]{1,0:T(8,128)S(1)} custom-call(f32[64,512]{1,0:T(8,128)S(1)} %get-tuple-element.11.slab_ref, f32[64,2048]{1,0:T(8,128)S(1)} %get-tuple-element.12.points_ref, f32[1,64]{1,0:T(1,128)S(1)} %get-tuple-element.13.inv_ref, bf16[2048,512]{1,0:T(8,128)(2,1)S(1)} %get-tuple-element.14.high_ref, ...), custom_call_target="tpu_custom_call" | custom-call | flops 2000000000 | bytes 5000000 | tf_op jit(solution)/shard_map/point_terms/pallas_call | solution.py:144
  9.0 0.1 collective-permute-start.4
  9.1 1.3 %collective-permute-done = f32[64,512]{1,0:T(8,128)S(1)} collective-permute-done((f32[64,512]{1,0:T(8,128)S(1)}, f32[64,512]{1,0:T(8,128)S(1)}, u32[]{:S(2)}, u32[]{:S(2)}) %collective-permute-start) | collective-permute-done | bytes 131104 | tf_op jit(solution)/shard_map/ppermute | solution.py:183
  10.4 2.0 %collective-permute-start.1 = (f32[64,512]{1,0:T(8,128)S(1)}, f32[64,512]{1,0:T(8,128)S(1)}, u32[]{:S(2)}, u32[]{:S(2)}) collective-permute-start(f32[64,512]{1,0:T(8,128)S(1)} %add.15), channel_id=1, source_target_pairs={{0,2},{1,9},{2,0},{3,11},{4,6},{5,13},{6,4},{7,15},{8,24},{9,1},{1... | collective-permute-start | bytes 393224 | tf_op jit(solution)/shard_map/ppermute | solution.py:183
  12.4 3.0 %collective-permute-done.1 = f32[64,512]{1,0:T(8,128)S(1)} collective-permute-done((f32[64,512]{1,0:T(8,128)S(1)}, f32[64,512]{1,0:T(8,128)S(1)}, u32[]{:S(2)}, u32[]{:S(2)}) %collective-permute-start.1) | collective-permute-done | bytes 131104 | tf_op jit(solution)/shard_map/ppermute | solution.py:183
  15.5 2.0 %collective-permute-start.2 = (f32[64,512]{1,0:T(8,128)S(1)}, f32[64,512]{1,0:T(8,128)S(1)}, u32[]{:S(2)}, u32[]{:S(2)}) collective-permute-start(f32[64,512]{1,0:T(8,128)S(1)} %add.16), channel_id=1, source_target_pairs={{0,4},{1,5},{2,6},{3,7},{4,0},{5,1},{6,2},{7,3},{8,10},{9,13},{10,... | collective-permute-start | bytes 393224 | tf_op jit(solution)/shard_map/ppermute | solution.py:183
  17.5 3.0 %collective-permute-done.2 = f32[64,512]{1,0:T(8,128)S(1)} collective-permute-done((f32[64,512]{1,0:T(8,128)S(1)}, f32[64,512]{1,0:T(8,128)S(1)}, u32[]{:S(2)}, u32[]{:S(2)}) %collective-permute-start.2) | collective-permute-done | bytes 131104 | tf_op jit(solution)/shard_map/ppermute | solution.py:183
  20.5 3.1 %collective-permute-start.3 = (f32[64,512]{1,0:T(8,128)S(1)}, f32[64,512]{1,0:T(8,128)S(1)}, u32[]{:S(2)}, u32[]{:S(2)}) collective-permute-start(f32[64,512]{1,0:T(8,128)S(1)} %add.17), channel_id=1, source_target_pairs={{0,16},{1,17},{2,18},{3,19},{4,20},{5,21},{6,22},{7,23},{8,12},{9,... | collective-permute-start | bytes 393224 | tf_op jit(solution)/shard_map/ppermute | solution.py:183
  23.6 0.0 collective-permute-done.4
  23.6 0.8 %add.18 = f32[64,2048]{1,0:T(8,128)} add(f32[64,2048]{1,0:T(8,128)S(1)} %point_terms.1, f32[64,2048]{1,0:T(8,128)S(1)} %collective-permute-done.4) | non-fusion elementwise | flops 131072 | bytes 1572864 | tf_op jit(solution)/shard_map/add | solution.py:163
  24.5 2.1 %collective-permute-done.3 = f32[64,512]{1,0:T(8,128)S(1)} collective-permute-done((f32[64,512]{1,0:T(8,128)S(1)}, f32[64,512]{1,0:T(8,128)S(1)}, u32[]{:S(2)}, u32[]{:S(2)}) %collective-permute-start.3) | collective-permute-done | bytes 131104 | tf_op jit(solution)/shard_map/ppermute | solution.py:183
  26.6 0.7 %add.19 = f32[64,512]{1,0:T(8,128)} add(f32[64,512]{1,0:T(8,128)S(1)} %add.17, f32[64,512]{1,0:T(8,128)S(1)} %collective-permute-done.3) | non-fusion elementwise | flops 32768 | bytes 393216 | tf_op jit(solution)/shard_map/add | solution.py:186
  (3 shorter events, 0.1 us)
Async XLA Ops:
  4.4 6.0 %collective-permute-start = (f32[64,512]{1,0:T(8,128)S(1)}, f32[64,512]{1,0:T(8,128)S(1)}, u32[]{:S(2)}, u32[]{:S(2)}) collective-permute-start(f32[64,512]{1,0:T(8,128)S(1)} %get-tuple-element.10), channel_id=1, source_target_pairs={{0,8},{1,3},{2,10},{3,1},{4,12},{5,7},{6,14},{7,5},{8,0},{9,11},{1... | collective-permute-start | bytes 393224 | tf_op jit(solution)/shard_map/ppermute | solution.py:183
  9.0 14.6 %collective-permute-start.4 = (f32[64,2048]{1,0:T(8,128)S(1)}, f32[64,2048]{1,0:T(8,128)S(1)}, u32[]{:S(2)}, u32[]{:S(2)}) collective-permute-start(f32[64,2048]{1,0:T(8,128)S(1)} %point_terms.1), channel_id=1, source_target_pairs={{0,1},{1,0},{2,3},{3,2},{4,5},{5,4},{6,7},{7,6},{8,9},{9,8},{10,11... | collective-permute-start | bytes 1572872 | tf_op jit(solution)/shard_map/ppermute | solution.py:160
  10.4 5.0 %collective-permute-start.1 = (f32[64,512]{1,0:T(8,128)S(1)}, f32[64,512]{1,0:T(8,128)S(1)}, u32[]{:S(2)}, u32[]{:S(2)}) collective-permute-start(f32[64,512]{1,0:T(8,128)S(1)} %add.15), channel_id=1, source_target_pairs={{0,2},{1,9},{2,0},{3,11},{4,6},{5,13},{6,4},{7,15},{8,24},{9,1},{1... | collective-permute-start | bytes 393224 | tf_op jit(solution)/shard_map/ppermute | solution.py:183
  15.5 5.0 %collective-permute-start.2 = (f32[64,512]{1,0:T(8,128)S(1)}, f32[64,512]{1,0:T(8,128)S(1)}, u32[]{:S(2)}, u32[]{:S(2)}) collective-permute-start(f32[64,512]{1,0:T(8,128)S(1)} %add.16), channel_id=1, source_target_pairs={{0,4},{1,5},{2,6},{3,7},{4,0},{5,1},{6,2},{7,3},{8,10},{9,13},{10,... | collective-permute-start | bytes 393224 | tf_op jit(solution)/shard_map/ppermute | solution.py:183
  20.5 6.1 %collective-permute-start.3 = (f32[64,512]{1,0:T(8,128)S(1)}, f32[64,512]{1,0:T(8,128)S(1)}, u32[]{:S(2)}, u32[]{:S(2)}) collective-permute-start(f32[64,512]{1,0:T(8,128)S(1)} %add.17), channel_id=1, source_target_pairs={{0,16},{1,17},{2,18},{3,19},{4,20},{5,21},{6,22},{7,23},{8,12},{9,... | collective-permute-start | bytes 393224 | tf_op jit(solution)/shard_map/ppermute | solution.py:183
